TPU v7x, 32 devices: a whole 2x2x4 slice. The times are simulated.
32 devices in a mesh: circ: 8 (over z, core), axial: 4 (over y, x).
Axes of the slice: x: 2, y: 2, z: 4, core: 2. Of those that a mesh axis runs over, the one named last changes fastest.
Arguments:
- interior_inv: bfloat16 [8, 4, 8, 512, 512], P('circ', 'axial'), as said below
- coupling: bfloat16 [8, 4, 8, 512, 640], P('circ', 'axial'), may hold values from -0.25 to 0.25
- boundary_diag: bfloat16 [8, 4, 8, 5, 128, 128], P('circ', 'axial'), may hold values from -3 to 3
- directions: int32 [8, 4, 8, 5], P('circ', 'axial'), may hold values from 0 to 4, as said below
- slot_ids: int32 [8, 4, 8, 5], P('circ', 'axial'), may hold values from 0 to 7, as said below
- live_blocks: int32 [8, 4, 8], P('circ', 'axial'), may hold values from 1 to 5, as said below
- weights: int32 [8, 4, 8, 5], P('circ', 'axial'), may hold values from 1 to 4
Outputs:
- averaged: float32 [8, 4, 8, 128, 128], P('circ', 'axial')
- deviation: bfloat16 [8, 4, 8, 5, 128, 128], P('circ', 'axial')
Inputs may be any that keep to these rules, and one draw needn't show every extreme that they name: `directions`: 0 to 4; never 3 on the last device row along axial, never 4 on the first. `slot_ids`: the slot 7 is named on every device. `live_blocks`: the first subdomain of the first device has all 5 blocks live. `interior_inv`: symmetric.
All inputs are finite; a program needn't handle non-finite values.
Results may differ from a plain program's by a relative error of at most 0.007.
Values may be sent and summed in bfloat16 or wider, within the bound.
No kernel may reach another device: no remote copies, remote signals or barrier semaphores. Data moves between devices by JAX's collectives and lax.ppermute only.
A program may use at most 128 MiB of HBM per device.

v0:
```python
import jax
import jax.numpy as jnp
from jax import lax
from jax.sharding import PartitionSpec as P

NI = 512
NBLK = 5
BS = 128
OWN = 8


def as_sent(x):

    def short(part):
        return part.astype(jnp.bfloat16) if part.dtype == jnp.float32 else part

    return jax.tree.map(short, x)


def from_behind(x, axis, by):
    count = lax.axis_size(axis)
    return lax.ppermute(x, axis, [(i, (i + by) % count) for i in range(count)])


def from_behind_2(value, axis, steps):
    count = lax.axis_size(axis)
    first, last = (max(0, -steps), min(count, count - steps))
    return lax.ppermute(value, axis, [(source, source + steps) for source in range(first, last)])


def padded_2(block, sides, width):
    for axis, dim in sides:
        count = lax.axis_size(axis)
        forward = [(i, i + 1) for i in range(count - 1)]
        forward.append((count - 1, 0))
        backward = [(target, source) for source, target in forward]
        low = lax.ppermute(
            lax.slice_in_dim(block, block.shape[dim] - width, None, axis=dim), axis, forward
        )
        high = lax.ppermute(lax.slice_in_dim(block, 0, width, axis=dim), axis, backward)
        block = jnp.concatenate([low, block, high], axis=dim)
    return block


def presum(routing, blocks):
    contrib = jnp.einsum("sno,snxy->oxy", routing, blocks, preferred_element_type=jnp.float32)
    return (contrib, jnp.sum(routing.astype(jnp.float32), axis=(0, 1)))


def body(interior_inv, coupling, boundary_diag, directions, slot_ids, live_blocks, weights):
    inverse = interior_inv[0, 0]
    coupled = coupling[0, 0]
    subs = coupled.shape[0]
    solved = jnp.einsum(
        "sij,sjk->sik", inverse, coupled, preferred_element_type=jnp.float32
    ).astype(jnp.bfloat16)
    left = coupled.reshape(subs, NI, NBLK, BS)
    right = solved.reshape(subs, NI, NBLK, BS)
    trailing = jnp.einsum("sinx,siny->snxy", left, right, preferred_element_type=jnp.float32)
    schur = (boundary_diag[0, 0].astype(jnp.float32) - trailing).astype(jnp.bfloat16)
    codes = directions[0, 0]
    slots = slot_ids[0, 0]
    live_mask = jnp.arange(NBLK)[None, :] < live_blocks[0, 0][:, None]
    onehot = slots[..., None] == jnp.arange(OWN)[None, None, :]
    scaled = weights[0, 0].astype(jnp.float32)

    def route(code):
        chosen = (live_mask & (codes == code)).astype(jnp.float32) * scaled
        return (onehot.astype(jnp.float32) * chosen[..., None]).astype(jnp.bfloat16)

    total_sum, weight_sum = presum(route(0), schur)
    for offset, code in ((1, 1), (-1, 2)):
        portion, counts = from_behind(as_sent(presum(route(code), schur)), "circ", offset)
        total_sum = total_sum + portion
        weight_sum = weight_sum + counts
    for offset, code in ((1, 3), (-1, 4)):
        portion, counts = from_behind_2(as_sent(presum(route(code), schur)), "axial", offset)
        total_sum = total_sum + portion
        weight_sum = weight_sum + counts
    averaged = total_sum / jnp.maximum(weight_sum, 1.0)[:, None, None]
    padded = padded_2(
        averaged[None, None].astype(jnp.bfloat16), (("circ", 0), ("axial", 1)), 1
    ).astype(jnp.float32)
    stacked = jnp.stack([averaged, padded[2, 1], padded[0, 1], padded[1, 2], padded[1, 0]])
    fetched = stacked[codes, slots]
    deviation = jnp.where(
        live_mask[..., None, None], schur.astype(jnp.float32) - fetched, 0.0
    ).astype(jnp.bfloat16)
    return (averaged[None, None], deviation[None, None])


def solution(mesh):
    return jax.shard_map(
        body,
        mesh=mesh,
        in_specs=(
            P("circ", "axial", None, None, None),
            P("circ", "axial", None, None, None),
            P("circ", "axial", None, None, None, None),
            P("circ", "axial", None, None),
            P("circ", "axial", None, None),
            P("circ", "axial", None),
            P("circ", "axial", None, None),
        ),
        out_specs=(
            P("circ", "axial", None, None, None),
            P("circ", "axial", None, None, None, None),
        ),
        check_vma=False,
    )
```

profile of v0, /device:TPU:0, one launch (start us, length us, event | category | flops | bytes accessed | tf_op | source)
XLA Modules:
  0.0 135.9 jit_solution(1436093374274775297)
XLA Ops:
  4.6 7.9 %copy.41 = bf16[1,1,8,512,640]{3,4,2,1,0:T(8,128)(2,1)} copy(bf16[1,1,8,512,640]{4,3,2,1,0:T(8,128)(2,1)} %param.8) | data formatting | bytes 10485760 | tf_op args[1]
  12.5 9.6 %fusion.3 = bf16[8,512,640]{2,1,0:T(8,128)(2,1)} fusion(bf16[1,1,8,512,640]{4,3,2,1,0:T(8,128)(2,1)} %param.8, bf16[1,1,8,512,512]{4,3,2,1,0:T(8,128)(2,1)} %param.7), kind=kOutput, calls=%fused_computation.4 | convolution fusion | flops 2686976000 | bytes 14680064 | tf_op jit(solution)/shard_map/sij,sjk->sik/dot_general | solution.py:54
  22.0 8.0 %copy.40 = bf16[8,512,640]{1,2,0:T(8,128)(2,1)} copy(bf16[8,512,640]{2,1,0:T(8,128)(2,1)} %fusion.3) | data formatting | bytes 10485760 | tf_op jit(solution)/shard_map/convert_element_type | solution.py:56
  30.8 5.6 %fusion.8 = bf16[8,5,128,128]{2,3,1,0:T(8,128)(2,1)S(1)} fusion(bf16[8,512,5,128]{1,3,2,0:T(8,128)(2,1)} %bitcast.118, bf16[8,512,5,128]{1,3,2,0:T(8,128)(2,1)} %bitcast.117, bf16[1,1,8,5,128,128]{4,5,3,2,1,0:T(8,128)(2,1)S(1)} %copy.39), kind=kOutput, calls=%fused_computation.6 | convolution fusion | flops 673054720 | bytes 13107200 | tf_op jit(solution)/shard_map/sinx,siny->snxy/dot_general | solution.py:59
  36.4 1.3 copy.43
  38.3 2.7 %collective-permute-start = (bf16[8,128,128]{2,0,1:T(8,128)(2,1)S(1)}, bf16[8,128,128]{2,0,1:T(8,128)(2,1)}, u32[]{:S(2)}, u32[]{:S(2)}) collective-permute-start(bf16[8,128,128]{2,0,1:T(8,128)(2,1)S(1)} %fusion.10), channel_id=1, source_target_pairs={{0,4},{4,8},{8,12},{12,16},{16,20},{20,24},{24,28},{28,0},{1,5},{5... | collective-permute-start | bytes 786440 | tf_op jit(solution)/shard_map/ppermute | solution.py:22
  41.6 1.4 %collective-permute-start.1 = (bf16[8,128,128]{2,0,1:T(8,128)(2,1)S(1)}, bf16[8,128,128]{2,0,1:T(8,128)(2,1)}, u32[]{:S(2)}, u32[]{:S(2)}) collective-permute-start(bf16[8,128,128]{2,0,1:T(8,128)(2,1)S(1)} %fusion.11), channel_id=1, source_target_pairs={{0,28},{4,0},{8,4},{12,8},{16,12},{20,16},{24,20},{28,24},{1,29},{... | collective-permute-start | bytes 786440 | tf_op jit(solution)/shard_map/ppermute | solution.py:22
  43.7 4.6 %collective-permute-start.2 = (bf16[8,128,128]{2,0,1:T(8,128)(2,1)S(1)}, bf16[8,128,128]{2,0,1:T(8,128)(2,1)}, u32[]{:S(2)}, u32[]{:S(2)}) collective-permute-start(bf16[8,128,128]{2,0,1:T(8,128)(2,1)S(1)} %fusion.12), channel_id=1, source_target_pairs={{0,1},{1,2},{2,3},{4,5},{5,6},{6,7},{8,9},{9,10},{10,11},{12,13},{... | collective-permute-start | bytes 786440 | tf_op jit(solution)/shard_map/ppermute | solution.py:28
  48.3 1.3 fusion.13
  49.6 1.3 collective-permute-start.3
  51.3 1.3 collective-permute-done.5
  52.6 4.3 %collective-permute-start.6 = (bf16[8]{0:T(256)(128)(2,1)S(1)}, bf16[8]{0:T(256)(128)(2,1)S(1)}, u32[]{:S(2)}, u32[]{:S(2)}) collective-permute-start(bf16[8]{0:T(256)(128)(2,1)S(1)} %get-tuple-element.8), channel_id=1, source_target_pairs={{0,1},{1,2},{2,3},{4,5},{5,6},{6,7},{8,9},{9,10},{10,11},{12,13},{... | collective-permute-start | bytes 56 | tf_op jit(solution)/shard_map/ppermute | solution.py:28
  57.0 1.3 collective-permute-done.6
  58.2 1.3 collective-permute-start.7
  59.5 4.4 %collective-permute-done.7 = bf16[8]{0:T(256)(128)(2,1)S(1)} collective-permute-done((bf16[8]{0:T(256)(128)(2,1)S(1)}, bf16[8]{0:T(256)(128)(2,1)S(1)}, u32[]{:S(2)}, u32[]{:S(2)}) %collective-permute-start.7) | collective-permute-done | bytes 48 | tf_op jit(solution)/shard_map/ppermute | solution.py:28
  64.0 2.6 %bitcast_dynamic-update-slice_fusion.1 = (f32[5,8,128,128]{3,1,2,0:T(8,128)}, f32[8,128,128]{2,0,1:T(8,128)S(1)}) fusion(f32[8]{0:T(128)S(1)} %add_maximum_fusion, bf16[8,128,128]{2,0,1:T(8,128)(2,1)} %collective-permute-done.3, bf16[8,128,128]{2,0,1:T(8,128)(2,1)} %collective-permute-done.2, bf16[8,128,128]{2,0,1:T(8,128)(2,1)} %collective-permute-done.1, ...), kind=kOutput, calls=%fused_computation.26 | convolution fusion | flops 11666047 | bytes 3408144 | tf_op jit(solution)/shard_map/sno,snxy->oxy/dot_general | solution.py:46
  66.7 3.5 %collective-permute-start.9 = (bf16[1,1,8,128,128]{4,2,3,1,0:T(8,128)(2,1)S(1)}, bf16[1,1,8,128,128]{4,2,3,1,0:T(8,128)(2,1)S(1)}, u32[]{:S(2)}, u32[]{:S(2)}) collective-permute-start(bf16[1,1,8,128,128]{4,2,3,1,0:T(8,128)(2,1)S(1)} %convert_bitcast_fusion.3), channel_id=1, source_target_pairs={{4,0},{8,4},{12,8},{16,12},{20,16},{24,20},{28,24},{0,28},{5,1},{9... | collective-permute-start | bytes 786440 | tf_op jit(solution)/shard_map/ppermute | solution.py:40
  70.2 6.6 %collective-permute-done.8 = bf16[1,1,8,128,128]{4,2,3,1,0:T(8,128)(2,1)S(1)} collective-permute-done((bf16[1,1,8,128,128]{4,2,3,1,0:T(8,128)(2,1)S(1)}, bf16[1,1,8,128,128]{4,2,3,1,0:T(8,128)(2,1)S(1)}, u32[]{:S(2)}, u32[]{:S(2)}) %collective-permute-start.8) | collective-permute-done | bytes 262176 | tf_op jit(solution)/shard_map/ppermute | solution.py:37
  77.5 1.0 pad_maximum_fusion
  78.4 2.9 %collective-permute-start.10 = (bf16[3,1,8,128,128]{4,2,3,1,0:T(8,128)(2,1)}, bf16[3,1,8,128,128]{4,2,3,1,0:T(8,128)(2,1)S(1)}, u32[]{:S(2)}, u32[]{:S(2)}) collective-permute-start(bf16[3,1,8,128,128]{4,2,3,1,0:T(8,128)(2,1)} %pad_maximum_fusion), channel_id=1, source_target_pairs={{0,1},{1,2},{2,3},{3,0},{4,5},{5,6},{6,7},{7,4},{8,9},{9,10},{10,1... | collective-permute-start | bytes 2359304 | tf_op jit(solution)/shard_map/ppermute | solution.py:37
  81.6 2.0 %copy.59 = f32[1,1,8,128,128]{4,3,2,1,0:T(8,128)} copy(f32[1,1,8,128,128]{4,2,3,1,0:T(8,128)} %bitcast.120) | data formatting | bytes 1048576
  83.6 16.4 %collective-permute-done.10 = bf16[3,1,8,128,128]{4,2,3,1,0:T(8,128)(2,1)S(1)} collective-permute-done((bf16[3,1,8,128,128]{4,2,3,1,0:T(8,128)(2,1)}, bf16[3,1,8,128,128]{4,2,3,1,0:T(8,128)(2,1)S(1)}, u32[]{:S(2)}, u32[]{:S(2)}) %collective-permute-start.10) | collective-permute-done | bytes 786464 | tf_op jit(solution)/shard_map/ppermute | solution.py:37
  100.0 17.0 %collective-permute-done.11 = bf16[3,1,8,128,128]{4,2,3,1,0:T(8,128)(2,1)S(1)} collective-permute-done((bf16[3,1,8,128,128]{4,2,3,1,0:T(8,128)(2,1)}, bf16[3,1,8,128,128]{4,2,3,1,0:T(8,128)(2,1)S(1)}, u32[]{:S(2)}, u32[]{:S(2)}) %collective-permute-start.11) | collective-permute-done | bytes 786464 | tf_op jit(solution)/shard_map/ppermute | solution.py:40
  117.0 1.8 %fusion.16 = f32[5,8,128,128]{3,1,2,0:T(8,128)} fusion(f32[5,8,128,128]{3,1,2,0:T(8,128)} %get-tuple-element.15, bf16[3,1,8,128,128]{4,2,3,1,0:T(8,128)(2,1)S(1)} %collective-permute-done.11, bf16[3,1,8,128,128]{4,2,3,1,0:T(8,128)(2,1)S(1)} %collective-permute-done.10, bf16[1,1,8,128,128]{4,2,3,1,0:T(8,128)(2,1)} %copy-done, ...), kind=kLoop, calls=%fused_computation.24 | loop fusion | flops 1310720 | bytes 2883584
  118.7 0.8 fusion.15
  119.6 0.8 fusion.14
  120.4 0.8 bitcast_dynamic-update-slice_fusion
  121.3 3.7 %copy.57 = f32[5,8,128,128]{3,2,1,0:T(8,128)} copy(f32[5,8,128,128]{3,1,2,0:T(8,128)} %bitcast_dynamic-update-slice_fusion) | data formatting | bytes 5242880 | tf_op jit(solution)/shard_map/stack | solution.py:84
  125.0 4.1 %gather_fusion = f32[40,128,128]{2,1,0:T(8,128)} fusion(f32[5,8,128,128]{3,2,1,0:T(8,128)} %copy.57, s32[40]{0:T(128)S(1)} %reshape.264), kind=kCustom, calls=%fused_computation | custom fusion | bytes 5243200 | tf_op jit(solution)/shard_map/gather | solution.py:85
  129.1 3.2 %copy.58 = f32[40,128,128]{1,2,0:T(8,128)} copy(f32[40,128,128]{2,1,0:T(8,128)} %gather_fusion) | data formatting | bytes 5242880 | tf_op jit(solution)/shard_map/gather | solution.py:85
  132.3 2.1 %fusion.9 = bf16[1,1,8,5,128,128]{4,5,3,2,1,0:T(8,128)(2,1)S(1)} fusion(f32[8,5,128,128]{2,3,1,0:T(8,128)} %bitcast.119, bf16[8,5,128,128]{2,3,1,0:T(8,128)(2,1)S(1)} %fusion.8, pred[8,5]{1,0:T(8,128)(4,1)S(1)} %iota_compare_fusion.1), kind=kLoop, calls=%fused_computation.8 | loop fusion | flops 2621440 | bytes 5242920 | tf_op jit(solution)/shard_map/broadcast_in_dim | solution.py:89
  134.5 1.4 %copy.60 = bf16[1,1,8,5,128,128]{5,4,3,2,1,0:T(8,128)(2,1)} copy(bf16[1,1,8,5,128,128]{4,5,3,2,1,0:T(8,128)(2,1)S(1)} %fusion.9) | data formatting | bytes 2621440
  (45 shorter events, 8.1 us)
Async XLA Ops:
  4.1 47.0 %collective-permute-start.4 = (bf16[8]{0:T(256)(128)(2,1)S(1)}, bf16[8]{0:T(256)(128)(2,1)S(1)}, u32[]{:S(2)}, u32[]{:S(2)}) collective-permute-start(bf16[8]{0:T(256)(128)(2,1)S(1)} %get-tuple-element.6), channel_id=1, source_target_pairs={{0,4},{4,8},{8,12},{12,16},{16,20},{20,24},{24,28},{28,0},{1,5},{5... | collective-permute-start | bytes 56 | tf_op jit(solution)/shard_map/ppermute | solution.py:22
  22.0 8.0 %copy-start.3 = (bf16[1,1,8,5,128,128]{5,4,3,2,1,0:T(8,128)(2,1)S(1)}, bf16[1,1,8,5,128,128]{5,4,3,2,1,0:T(8,128)(2,1)}, u32[]{:S(2)}) copy-start(bf16[1,1,8,5,128,128]{5,4,3,2,1,0:T(8,128)(2,1)} %param.9) | copy-start | bytes 3932164
  38.3 25.6 %collective-permute-start = (bf16[8,128,128]{2,0,1:T(8,128)(2,1)S(1)}, bf16[8,128,128]{2,0,1:T(8,128)(2,1)}, u32[]{:S(2)}, u32[]{:S(2)}) collective-permute-start(bf16[8,128,128]{2,0,1:T(8,128)(2,1)S(1)} %fusion.10), channel_id=1, source_target_pairs={{0,4},{4,8},{8,12},{12,16},{16,20},{20,24},{24,28},{28,0},{1,5},{5... | collective-permute-start | bytes 786440 | tf_op jit(solution)/shard_map/ppermute | solution.py:22
  41.6 22.3 %collective-permute-start.1 = (bf16[8,128,128]{2,0,1:T(8,128)(2,1)S(1)}, bf16[8,128,128]{2,0,1:T(8,128)(2,1)}, u32[]{:S(2)}, u32[]{:S(2)}) collective-permute-start(bf16[8,128,128]{2,0,1:T(8,128)(2,1)S(1)} %fusion.11), channel_id=1, source_target_pairs={{0,28},{4,0},{8,4},{12,8},{16,12},{20,16},{24,20},{28,24},{1,29},{... | collective-permute-start | bytes 786440 | tf_op jit(solution)/shard_map/ppermute | solution.py:22
  43.7 20.3 %collective-permute-start.2 = (bf16[8,128,128]{2,0,1:T(8,128)(2,1)S(1)}, bf16[8,128,128]{2,0,1:T(8,128)(2,1)}, u32[]{:S(2)}, u32[]{:S(2)}) collective-permute-start(bf16[8,128,128]{2,0,1:T(8,128)(2,1)S(1)} %fusion.12), channel_id=1, source_target_pairs={{0,1},{1,2},{2,3},{4,5},{5,6},{6,7},{8,9},{9,10},{10,11},{12,13},{... | collective-permute-start | bytes 786440 | tf_op jit(solution)/shard_map/ppermute | solution.py:28
  49.6 14.4 %collective-permute-start.3 = (bf16[8,128,128]{2,0,1:T(8,128)(2,1)}, bf16[8,128,128]{2,0,1:T(8,128)(2,1)}, u32[]{:S(2)}, u32[]{:S(2)}) collective-permute-start(bf16[8,128,128]{2,0,1:T(8,128)(2,1)} %fusion.13), channel_id=1, source_target_pairs={{1,0},{2,1},{3,2},{5,4},{6,5},{7,6},{9,8},{10,9},{11,10},{13,12},{... | collective-permute-start | bytes 786440 | tf_op jit(solution)/shard_map/ppermute | solution.py:28
  51.1 1.6 %collective-permute-start.5 = (bf16[8]{0:T(256)(128)(2,1)S(1)}, bf16[8]{0:T(256)(128)(2,1)S(1)}, u32[]{:S(2)}, u32[]{:S(2)}) collective-permute-start(bf16[8]{0:T(256)(128)(2,1)S(1)} %get-tuple-element.7), channel_id=1, source_target_pairs={{0,28},{4,0},{8,4},{12,8},{16,12},{20,16},{24,20},{28,24},{1,29},{... | collective-permute-start | bytes 56 | tf_op jit(solution)/shard_map/ppermute | solution.py:22
  52.6 5.6 %collective-permute-start.6 = (bf16[8]{0:T(256)(128)(2,1)S(1)}, bf16[8]{0:T(256)(128)(2,1)S(1)}, u32[]{:S(2)}, u32[]{:S(2)}) collective-permute-start(bf16[8]{0:T(256)(128)(2,1)S(1)} %get-tuple-element.8), channel_id=1, source_target_pairs={{0,1},{1,2},{2,3},{4,5},{5,6},{6,7},{8,9},{9,10},{10,11},{12,13},{... | collective-permute-start | bytes 56 | tf_op jit(solution)/shard_map/ppermute | solution.py:28
  58.2 5.7 %collective-permute-start.7 = (bf16[8]{0:T(256)(128)(2,1)S(1)}, bf16[8]{0:T(256)(128)(2,1)S(1)}, u32[]{:S(2)}, u32[]{:S(2)}) collective-permute-start(bf16[8]{0:T(256)(128)(2,1)S(1)} %get-tuple-element.9), channel_id=1, source_target_pairs={{1,0},{2,1},{3,2},{5,4},{6,5},{7,6},{9,8},{10,9},{11,10},{13,12},{... | collective-permute-start | bytes 56 | tf_op jit(solution)/shard_map/ppermute | solution.py:28
  63.9 17.4 %copy-start.4 = (s32[1,1,8,5]{2,1,3,0:T(1,128)S(1)}, s32[1,1,8,5]{2,1,3,0:T(1,128)}, u32[]{:S(2)}) copy-start(s32[1,1,8,5]{2,1,3,0:T(1,128)} %param.10) | copy-start | bytes 484
  63.9 17.4 %copy-start.5 = (s32[1,1,8,5]{2,1,3,0:T(1,128)S(1)}, s32[1,1,8,5]{2,1,3,0:T(1,128)}, u32[]{:S(2)}) copy-start(s32[1,1,8,5]{2,1,3,0:T(1,128)} %param.11) | copy-start | bytes 484
  63.9 17.6 %copy-start.6 = (s32[1,1,8]{2,1,0:T(1,128)S(1)}, s32[1,1,8]{2,1,0:T(1,128)}, u32[]{:S(2)}) copy-start(s32[1,1,8]{2,1,0:T(1,128)} %param.12) | copy-start | bytes 100
  66.6 11.9 %copy-start.2 = (f32[8,128,128]{2,0,1:T(8,128)}, f32[8,128,128]{2,0,1:T(8,128)S(1)}, u32[]{:S(2)}) copy-start(f32[8,128,128]{2,0,1:T(8,128)S(1)} %get-tuple-element.16) | copy-start | bytes 1572868
  66.6 10.2 %collective-permute-start.8 = (bf16[1,1,8,128,128]{4,2,3,1,0:T(8,128)(2,1)S(1)}, bf16[1,1,8,128,128]{4,2,3,1,0:T(8,128)(2,1)S(1)}, u32[]{:S(2)}, u32[]{:S(2)}) collective-permute-start(bf16[1,1,8,128,128]{4,2,3,1,0:T(8,128)(2,1)S(1)} %convert_bitcast_fusion.3), channel_id=1, source_target_pairs={{0,4},{4,8},{8,12},{12,16},{16,20},{20,24},{24,28},{28,0},{1,5},{5... | collective-permute-start | bytes 786440 | tf_op jit(solution)/shard_map/ppermute | solution.py:37
  66.7 10.1 %collective-permute-start.9 = (bf16[1,1,8,128,128]{4,2,3,1,0:T(8,128)(2,1)S(1)}, bf16[1,1,8,128,128]{4,2,3,1,0:T(8,128)(2,1)S(1)}, u32[]{:S(2)}, u32[]{:S(2)}) collective-permute-start(bf16[1,1,8,128,128]{4,2,3,1,0:T(8,128)(2,1)S(1)} %convert_bitcast_fusion.3), channel_id=1, source_target_pairs={{4,0},{8,4},{12,8},{16,12},{20,16},{24,20},{28,24},{0,28},{5,1},{9... | collective-permute-start | bytes 786440 | tf_op jit(solution)/shard_map/ppermute | solution.py:40
  76.8 0.7 copy-start
  78.4 21.6 %collective-permute-start.10 = (bf16[3,1,8,128,128]{4,2,3,1,0:T(8,128)(2,1)}, bf16[3,1,8,128,128]{4,2,3,1,0:T(8,128)(2,1)S(1)}, u32[]{:S(2)}, u32[]{:S(2)}) collective-permute-start(bf16[3,1,8,128,128]{4,2,3,1,0:T(8,128)(2,1)} %pad_maximum_fusion), channel_id=1, source_target_pairs={{0,1},{1,2},{2,3},{3,0},{4,5},{5,6},{6,7},{7,4},{8,9},{9,10},{10,1... | collective-permute-start | bytes 2359304 | tf_op jit(solution)/shard_map/ppermute | solution.py:37
  81.3 35.6 %collective-permute-start.11 = (bf16[3,1,8,128,128]{4,2,3,1,0:T(8,128)(2,1)}, bf16[3,1,8,128,128]{4,2,3,1,0:T(8,128)(2,1)S(1)}, u32[]{:S(2)}, u32[]{:S(2)}) collective-permute-start(bf16[3,1,8,128,128]{4,2,3,1,0:T(8,128)(2,1)} %pad_maximum_fusion), channel_id=1, source_target_pairs={{1,0},{2,1},{3,2},{0,3},{5,4},{6,5},{7,6},{4,7},{9,8},{10,9},{11,1... | collective-permute-start | bytes 2359304 | tf_op jit(solution)/shard_map/ppermute | solution.py:40
  81.5 37.2 %copy-start.1 = (bf16[1,1,8,128,128]{4,2,3,1,0:T(8,128)(2,1)S(1)}, bf16[1,1,8,128,128]{4,2,3,1,0:T(8,128)(2,1)}, u32[]{:S(2)}) copy-start(bf16[1,1,8,128,128]{4,2,3,1,0:T(8,128)(2,1)} %copy-done) | copy-start | bytes 786436
where the time goes:
time: 137 us; the launch traced here: 136 us
  waiting for transfers between devices  46.9 us (34%)
  local copies, waits for them, and re-layouts  36 us (26%)
  starting transfers between devices  23 us (17%)
  matrix products  20.8 us (15%)
  other arithmetic  8.5 us (6%)
    ppermute x2, waiting for transfers between devices, padded_2(): lax.ppermute(lax.slice_in_dim(block, block.shape[dim] - width, None, axis...  23 us
    ppermute x2, waiting for transfers between devices, padded_2(): lax.ppermute(lax.slice_in_dim(block, 0, width, axis=dim), axis, backward)  17 us
    unnamed x20, local copies, waits for them, and re-layouts  14.3 us
    ppermute x4, starting transfers between devices, from_behind_2(): lax.ppermute(value, axis, [(source, source + steps) for source in range(f...  11.5 us
    dot_general x1, matrix products, body(): jnp.einsum('sij,sjk->sik', inverse, coupled, preferred_element_type=jnp.f...  9.57 us
    convert_element_type x1, local copies, waits for them, and re-layouts, body(): solved = jnp.einsum('sij,sjk->sik', inverse, coupled, preferred_element_t...  7.95 us
    gather x2, local copies, waits for them, and re-layouts, body(): fetched = stacked[codes, slots]  7.35 us
    ppermute x4, waiting for transfers between devices, from_behind_2(): lax.ppermute(value, axis, [(source, source + steps) for source in range(f...  5.65 us
  transfers between devices with their start and end apart: 12, of which 6 were waited for; matrix products, arithmetic and copies ran while one was open for 28% of the time, Pallas kernels for 0%

commit v1 on v0

v1 whole, which is shorter than its diff:
```python
import functools

import jax
import jax.numpy as jnp
from jax import lax
from jax.experimental import pallas as pl
from jax.experimental.pallas import tpu as pltpu
from jax.sharding import PartitionSpec as P

PAD = 16


def near_pairs(count):
    return [(i, i ^ 1) for i in range(count)]


def far_pairs(count, periodic):
    pairs = []
    for i in range(count):
        j = i + 1 if i % 2 else i - 1
        if periodic:
            pairs.append((i, j % count))
        elif 0 <= j < count:
            pairs.append((i, j))
    return pairs


def swap_all(to_near_c, to_far_c, to_near_a, to_far_a):
    circ, axial = lax.axis_size("circ"), lax.axis_size("axial")
    near_a = lax.ppermute(to_near_a, "axial", near_pairs(axial))
    far_c = lax.ppermute(to_far_c, "circ", far_pairs(circ, True))
    far_a = lax.ppermute(to_far_a, "axial", far_pairs(axial, False))
    near_c = lax.ppermute(to_near_c, "circ", near_pairs(circ))
    return near_c, far_c, near_a, far_a


def buffer_of(code):
    odd_c = lax.rem(lax.axis_index("circ"), 2)
    odd_a = lax.rem(lax.axis_index("axial"), 2)
    circ = jnp.where(odd_c == 0, code, 3 - code)
    axial = jnp.where(odd_a == 0, code, 7 - code)
    return jnp.where(code == 0, 0, jnp.where(code <= 2, circ, axial))


def schur_kernel(
    dirs, slots, live, weights, inv, coup, diag,
    schur, own, own_cnt, s1, s2, s3, s4,
    inv_v, coup_v, diag_v, acc, cnt, sems,
):
    subs, nblk, bs = diag.shape[0], diag.shape[1], diag.shape[2]
    own_slots = own.shape[0] // bs

    def loads(sub):
        pairs = ((coup, coup_v), (inv, inv_v), (diag, diag_v))
        return [
            pltpu.make_async_copy(a.at[sub], b.at[sub], sems.at[j, sub])
            for j, (a, b) in enumerate(pairs)
        ]

    for sub in range(subs):
        for copy in loads(sub):
            copy.start()
    acc[...] = jnp.zeros_like(acc)
    cnt[...] = jnp.zeros_like(cnt)

    def step(sub, carry):
        for copy in loads(sub):
            copy.wait()
        c = coup_v[sub]
        st = jnp.dot(c.T, inv_v[sub], preferred_element_type=jnp.float32).astype(jnp.bfloat16)
        for k in range(nblk):
            cols = slice(k * bs, (k + 1) * bs)
            trail = jnp.dot(st[cols], c[:, cols], preferred_element_type=jnp.float32)
            block = (diag_v[sub, k].astype(jnp.float32) - trail).astype(jnp.bfloat16)
            schur[sub, k] = block
            w = jnp.where(k < live[0, sub], weights[k, 0, sub], 0).astype(jnp.float32)
            buf, slot = buffer_of(dirs[k, 0, sub]), slots[k, 0, sub]
            acc[buf * own_slots + slot] += w * block.astype(jnp.float32)
            cnt[buf, pl.ds(slot, 1), :] += jnp.full((1, bs), w, jnp.float32)
        return carry

    lax.fori_loop(0, subs, step, 0)
    for o in range(own_slots):
        own[o * bs:(o + 1) * bs] = acc[o]
    own_cnt[...] = cnt[0]
    for b, out in enumerate((s1, s2, s3, s4), 1):
        for o in range(own_slots):
            out[o * bs:(o + 1) * bs] = acc[b * own_slots + o].astype(jnp.bfloat16)
        out[own_slots * bs:] = cnt[b].astype(jnp.bfloat16)


def average_kernel(own, own_cnt, r1, r2, r3, r4, avg, avg_short):
    bs = own.shape[1]
    own_slots = own.shape[0] // bs
    parts = (r1, r2, r3, r4)
    count = own_cnt[...]
    for r in parts:
        count = count + r[own_slots * bs:].astype(jnp.float32)
    scale = 1.0 / jnp.maximum(count, 1.0)
    for o in range(own_slots):
        rows = slice(o * bs, (o + 1) * bs)
        total = own[rows]
        for r in parts:
            total = total + r[rows].astype(jnp.float32)
        mean = total * scale[o:o + 1]
        avg[rows] = mean
        avg_short[rows] = mean.astype(jnp.bfloat16)


def deviation_kernel(dirs, slots, live, schur, avg, r1, r2, r3, r4, dev, table, stage, sems):
    subs, nblk, bs = schur.shape[0], schur.shape[1], schur.shape[2]
    own_slots = avg.shape[0] // bs
    for b, r in enumerate((avg, r1, r2, r3, r4)):
        for o in range(own_slots):
            table[b * own_slots + o] = r[o * bs:(o + 1) * bs]
    stores = []
    for s in range(subs):
        for k in range(nblk):
            at = buffer_of(dirs[k, 0, s]) * own_slots + slots[k, 0, s]
            diff = schur[s, k].astype(jnp.float32) - table[at].astype(jnp.float32)
            stage[s, k] = jnp.where(k < live[0, s], diff, 0.0).astype(jnp.bfloat16)
        stores.append(pltpu.make_async_copy(stage.at[s], dev.at[s], sems.at[s]))
        stores[-1].start()
    for copy in stores:
        copy.wait()


def body(interior_inv, coupling, boundary_diag, directions, slot_ids, live_blocks, weights):
    inv, coup, diag = interior_inv[0, 0], coupling[0, 0], boundary_diag[0, 0]
    subs, ni, nb = coup.shape
    nblk, bs = diag.shape[1], diag.shape[2]
    own_slots = 8
    by_block = lambda x: jnp.transpose(x[0], (2, 0, 1))
    dirs, slots, wts = by_block(directions), by_block(slot_ids), by_block(weights)
    live = live_blocks[0]
    f32, bf16 = jnp.float32, jnp.bfloat16
    rows = own_slots * bs
    smem = pl.BlockSpec(memory_space=pltpu.SMEM)
    vmem = pl.BlockSpec(memory_space=pltpu.VMEM)
    hbm = pl.BlockSpec(memory_space=pltpu.HBM)
    sent = jax.ShapeDtypeStruct((rows + PAD, bs), bf16)
    schur, own, own_cnt, s1, s2, s3, s4 = pl.pallas_call(
        schur_kernel,
        in_specs=[smem] * 4 + [hbm] * 3,
        out_specs=[vmem] * 7,
        out_shape=[
            jax.ShapeDtypeStruct((subs, nblk, bs, bs), bf16),
            jax.ShapeDtypeStruct((rows, bs), f32),
            jax.ShapeDtypeStruct((PAD, bs), f32),
        ] + [sent] * 4,
        scratch_shapes=[
            pltpu.VMEM(inv.shape, bf16),
            pltpu.VMEM(coup.shape, bf16),
            pltpu.VMEM(diag.shape, bf16),
            pltpu.VMEM((5 * own_slots, bs, bs), f32),
            pltpu.VMEM((5, PAD, bs), f32),
            pltpu.SemaphoreType.DMA((3, subs)),
        ],
        compiler_params=pltpu.CompilerParams(vmem_limit_bytes=56 * 2**20),
        name="schur_and_sums",
    )(dirs, slots, live, wts, inv, coup, diag)
    r1, r2, r3, r4 = swap_all(s1, s2, s3, s4)
    avg, avg_short = pl.pallas_call(
        average_kernel,
        in_specs=[vmem] * 6,
        out_specs=[vmem] * 2,
        out_shape=[
            jax.ShapeDtypeStruct((rows, bs), f32),
            jax.ShapeDtypeStruct((rows, bs), bf16),
        ],
        compiler_params=pltpu.CompilerParams(vmem_limit_bytes=16 * 2**20),
        name="average",
    )(own, own_cnt, r1, r2, r3, r4)
    n1, n2, n3, n4 = swap_all(avg_short, avg_short, avg_short, avg_short)
    dev = pl.pallas_call(
        deviation_kernel,
        in_specs=[smem] * 3 + [vmem] * 6,
        out_specs=hbm,
        out_shape=jax.ShapeDtypeStruct((subs, nblk, bs, bs), bf16),
        scratch_shapes=[
            pltpu.VMEM((5 * own_slots, bs, bs), bf16),
            pltpu.VMEM((subs, nblk, bs, bs), bf16),
            pltpu.SemaphoreType.DMA((subs,)),
        ],
        compiler_params=pltpu.CompilerParams(vmem_limit_bytes=16 * 2**20),
        name="deviation",
    )(dirs, slots, live, schur, avg_short, n1, n2, n3, n4)
    return avg.reshape(1, 1, own_slots, bs, bs), dev[None, None]


def solution(mesh):
    return jax.shard_map(
        body,
        mesh=mesh,
        in_specs=(
            P("circ", "axial", None, None, None),
            P("circ", "axial", None, None, None),
            P("circ", "axial", None, None, None, None),
            P("circ", "axial", None, None),
            P("circ", "axial", None, None),
            P("circ", "axial", None),
            P("circ", "axial", None, None),
        ),
        out_specs=(
            P("circ", "axial", None, None, None),
            P("circ", "axial", None, None, None, None),
        ),
        check_vma=False,
    )
```

time: 137 us -> 47.9 us (0.35)
  local copies, waits for them, and re-layouts: 36 us -> 1.76 us
  waiting for transfers between devices: 46.9 us -> 15.6 us
  matrix products: 20.8 us -> 0 us
  Pallas kernels: 0 us -> 12.6 us
  other arithmetic: 8.5 us -> 0 us
  starting transfers between devices: 23 us -> 16.9 us
    ppermute x12 -> x8, waiting for transfers between devices: 46.9 us -> 15.6 us  [the longest x2 11.3 us: swap_all(): near_a = lax.ppermute(to_near_a, 'axial', near_pairs(axial))]
    dot_general x7 -> x0, matrix products: 20.8 us -> none  [the longest x1 9.57 us: body(): jnp.einsum('sij,sjk->sik', inverse, coupled, preferred_element_type=jnp.f...]
    pallas_call x0 -> x3, Pallas kernels: none -> 12.6 us  [the longest x1 9.75 us: body(): pl.pallas_call(schur_kernel, in_specs=[smem] * 4 + [hbm] * 3, out_specs=[...]
    unnamed x20 -> x12, local copies, waits for them, and re-layouts: 14.3 us -> 1.76 us
    convert_element_type x2 -> x0, local copies, waits for them, and re-layouts: 9.27 us -> none  [the longest x1 7.95 us: body(): solved = jnp.einsum('sij,sjk->sik', inverse, coupled, preferred_element_t...]
    gather x2 -> x0, local copies, waits for them, and re-layouts: 7.35 us -> none  [body(): fetched = stacked[codes, slots]]
    ppermute x12 -> x8, starting transfers between devices: 23 us -> 16.9 us  [the longest x2 9.72 us: swap_all(): near_a = lax.ppermute(to_near_a, 'axial', near_pairs(axial))]
    another operation x1 -> x0, local copies, waits for them, and re-layouts: 3.72 us -> none  [body(): jnp.stack([averaged, padded[2, 1], padded[0, 1], padded[1, 2], padded[1,...]
  transfers between devices with their start and end apart: 12 -> 8, of which waited for: 6 -> 3; matrix products, arithmetic and copies ran while one was open for 28% -> 0% of each run, Pallas kernels for 0% -> 0%
where the time goes in v1:
time: 47.9 us; the launch traced here: 47.6 us
  starting transfers between devices  16.9 us (35%)
  waiting for transfers between devices  15.6 us (33%)
  Pallas kernels  12.6 us (26%)
  local copies, waits for them, and re-layouts  1.76 us (4%)
  between operations  0.73 us (2%)
    ppermute x2, waiting for transfers between devices, swap_all(): near_a = lax.ppermute(to_near_a, 'axial', near_pairs(axial))  11.3 us
    pallas_call x1, Pallas kernels, body(): pl.pallas_call(schur_kernel, in_specs=[smem] * 4 + [hbm] * 3, out_specs=[...  9.75 us
    ppermute x2, starting transfers between devices, swap_all(): near_a = lax.ppermute(to_near_a, 'axial', near_pairs(axial))  9.72 us
    ppermute x2, starting transfers between devices, swap_all(): far_c = lax.ppermute(to_far_c, 'circ', far_pairs(circ, True))  5.11 us
    ppermute x2, waiting for transfers between devices, swap_all(): far_c = lax.ppermute(to_far_c, 'circ', far_pairs(circ, True))  4.27 us
    pallas_call x1, Pallas kernels, body(): pl.pallas_call(deviation_kernel, in_specs=[smem] * 3 + [vmem] * 6, out_sp...  1.87 us
    unnamed x12, local copies, waits for them, and re-layouts  1.76 us
    ppermute x2, starting transfers between devices, swap_all(): far_a = lax.ppermute(to_far_a, 'axial', far_pairs(axial, False))  1.33 us
  transfers between devices with their start and end apart: 8, of which 3 were waited for; matrix products, arithmetic and copies ran while one was open for 0% of the time, Pallas kernels for 0%

profile of v1, /device:TPU:0, one launch (start us, length us, event | category | flops | bytes accessed | tf_op | source)
XLA Modules:
  0.0 47.6 jit_solution(11086171021796360277)
XLA Ops:
  0.6 0.0 copy-start.2
  0.6 0.0 copy-start.3
  0.7 0.0 copy-start.5
  0.7 9.7 %schur_and_sums.1 = (bf16[8,5,128,128]{3,2,1,0:T(8,128)(2,1)}, f32[1024,128]{1,0:T(8,128)}, f32[16,128]{1,0:T(8,128)}, bf16[1040,128]{1,0:T(8,128)(2,1)}, bf16[1...) custom-call(s32[5,1,8]{2,1,0:T(1,128)} %bitcast.15, s32[5,1,8]{2,1,0:T(1,128)} %bitcast.17, ...), custom_call_target="tpu_custom_call" | custom-call | tf_op jit(solution)/shard_map/schur_and_sums/pallas_call | solution.py:142
  10.4 0.0 copy-start
  10.4 0.5 %collective-permute-start = (bf16[1040,128]{1,0:T(8,128)(2,1)}, bf16[1040,128]{1,0:T(8,128)(2,1)S(1)}, u32[]{:S(2)}, u32[]{:S(2)}) collective-permute-start(bf16[1040,128]{1,0:T(8,128)(2,1)} %get-tuple-element.13), channel_id=1, source_target_pairs={{0,4},{4,0},{8,12},{12,8},{16,20},{20,16},{24,28},{28,24},{1,5},{5... | collective-permute-start | bytes 798728 | tf_op jit(solution)/shard_map/ppermute | solution.py:33
  10.9 4.7 %collective-permute-start.1 = (bf16[1040,128]{1,0:T(8,128)(2,1)}, bf16[1040,128]{1,0:T(8,128)(2,1)S(1)}, u32[]{:S(2)}, u32[]{:S(2)}) collective-permute-start(bf16[1040,128]{1,0:T(8,128)(2,1)} %get-tuple-element.14), channel_id=1, source_target_pairs={{0,28},{4,8},{8,4},{12,16},{16,12},{20,24},{24,20},{28,0},{1,29},{... | collective-permute-start | bytes 798728 | tf_op jit(solution)/shard_map/ppermute | solution.py:31
  15.7 1.5 %collective-permute-start.2 = (bf16[1040,128]{1,0:T(8,128)(2,1)}, bf16[1040,128]{1,0:T(8,128)(2,1)S(1)}, u32[]{:S(2)}, u32[]{:S(2)}) collective-permute-start(bf16[1040,128]{1,0:T(8,128)(2,1)} %get-tuple-element.15), channel_id=1, source_target_pairs={{0,1},{1,0},{2,3},{3,2},{4,5},{5,4},{6,7},{7,6},{8,9},{9,8},{10,11... | collective-permute-start | bytes 798728 | tf_op jit(solution)/shard_map/ppermute | solution.py:30
  17.1 0.7 %collective-permute-start.3 = (bf16[1040,128]{1,0:T(8,128)(2,1)}, bf16[1040,128]{1,0:T(8,128)(2,1)S(1)}, u32[]{:S(2)}, u32[]{:S(2)}) collective-permute-start(bf16[1040,128]{1,0:T(8,128)(2,1)} %get-tuple-element.16), channel_id=1, source_target_pairs={{1,2},{2,1},{5,6},{6,5},{9,10},{10,9},{13,14},{14,13},{17,18},{18,... | collective-permute-start | bytes 798728 | tf_op jit(solution)/shard_map/ppermute | solution.py:32
  17.8 0.0 collective-permute-done.r1
  17.8 4.3 %collective-permute-done.1.r2 = bf16[1040,128]{1,0:T(8,128)(2,1)S(1)} collective-permute-done((bf16[1040,128]{1,0:T(8,128)(2,1)}, bf16[1040,128]{1,0:T(8,128)(2,1)S(1)}, u32[]{:S(2)}, u32[]{:S(2)}) %collective-permute-start.1) | collective-permute-done | bytes 266272 | tf_op jit(solution)/shard_map/ppermute | solution.py:31
  22.1 1.9 %collective-permute-done.2.r3 = bf16[1040,128]{1,0:T(8,128)(2,1)S(1)} collective-permute-done((bf16[1040,128]{1,0:T(8,128)(2,1)}, bf16[1040,128]{1,0:T(8,128)(2,1)S(1)}, u32[]{:S(2)}, u32[]{:S(2)}) %collective-permute-start.2) | collective-permute-done | bytes 266272 | tf_op jit(solution)/shard_map/ppermute | solution.py:30
  24.0 0.0 collective-permute-done.3.r4
  24.0 0.0 copy-start.1
  24.0 1.0 %copy-done.1 = f32[1024,128]{1,0:T(8,128)S(1)} copy-done((f32[1024,128]{1,0:T(8,128)S(1)}, f32[1024,128]{1,0:T(8,128)}, u32[]{:S(2)}) %copy-start.1) | copy-done | bytes 524312
  25.0 0.0 copy-start.4
  25.0 0.7 %copy-done.4 = f32[16,128]{1,0:T(8,128)S(1)} copy-done((f32[16,128]{1,0:T(8,128)S(1)}, f32[16,128]{1,0:T(8,128)}, u32[]{:S(2)}) %copy-start.4) | copy-done | bytes 8216
  25.7 1.0 %average.1 = (f32[1024,128]{1,0:T(8,128)}, bf16[1024,128]{1,0:T(8,128)(2,1)S(1)}) custom-call(f32[1024,128]{1,0:T(8,128)S(1)} %copy-done.1, f32[16,128]{1,0:T(8,128)S(1)} %copy-done.4, bf16[1040,128]{1,0:T(8,128)(2,1)S(1)} %collective-permute-done.r1, bf16[1040,128]{1,0:T(8,128)(2,1)S(1)} %collective-permute-done.1.r2, ...), custom_call_target="tpu_custom_call" | custom-call | tf_op jit(solution)/shard_map/average/pallas_call | solution.py:163
  26.7 0.7 %collective-permute-start.7 = (bf16[1024,128]{1,0:T(8,128)(2,1)S(1)}, bf16[1024,128]{1,0:T(8,128)(2,1)S(1)}, u32[]{:S(2)}, u32[]{:S(2)}) collective-permute-start(bf16[1024,128]{1,0:T(8,128)(2,1)S(1)} %get-tuple-element.19.avg), channel_id=1, source_target_pairs={{1,2},{2,1},{5,6},{6,5},{9,10},{10,9},{13,14},{14,13},{17,18},{18,... | collective-permute-start | bytes 786440 | tf_op jit(solution)/shard_map/ppermute | solution.py:32
  27.4 8.2 %collective-permute-start.6 = (bf16[1024,128]{1,0:T(8,128)(2,1)S(1)}, bf16[1024,128]{1,0:T(8,128)(2,1)S(1)}, u32[]{:S(2)}, u32[]{:S(2)}) collective-permute-start(bf16[1024,128]{1,0:T(8,128)(2,1)S(1)} %get-tuple-element.19.avg), channel_id=1, source_target_pairs={{0,1},{1,0},{2,3},{3,2},{4,5},{5,4},{6,7},{7,6},{8,9},{9,8},{10,11... | collective-permute-start | bytes 786440 | tf_op jit(solution)/shard_map/ppermute | solution.py:30
  35.6 0.4 collective-permute-start.5
  36.0 0.3 collective-permute-start.4
  36.3 0.0 collective-permute-done.7.r4
  36.3 9.5 %collective-permute-done.6.r3 = bf16[1024,128]{1,0:T(8,128)(2,1)S(1)} collective-permute-done((bf16[1024,128]{1,0:T(8,128)(2,1)S(1)}, bf16[1024,128]{1,0:T(8,128)(2,1)S(1)}, u32[]{:S(2)}, u32[]{:S(2)}) %collective-permute-start.6) | collective-permute-done | bytes 262176 | tf_op jit(solution)/shard_map/ppermute | solution.py:30
  45.7 0.0 collective-permute-done.5.r2
  45.7 0.0 collective-permute-done.4.r1
  45.7 0.0 copy-done.2
  45.7 0.0 copy-done.3
  45.7 0.0 copy-done.5
  45.8 0.0 copy-done
  45.8 1.9 %deviation.1 = bf16[8,5,128,128]{3,2,1,0:T(8,128)(2,1)} custom-call(s32[5,1,8]{2,1,0:T(1,128)S(1)} %bitcast.16, s32[5,1,8]{2,1,0:T(1,128)S(1)} %bitcast.18, s32[1,8]{1,0:T(1,128)S(1)} %bitcast.20, bf16[8,5,128,128]{3,2,1,0:T(8,128)(2,1)S(1)} %copy-done, bf16[1024,128]{1,0:T(8,128)(2,1)S(1)} %get-tuple-element.19.avg, ...), custom_call_target="tpu_custom_call" | custom-call | tf_op jit(solution)/shard_map/deviation/pallas_call | solution.py:175
Async XLA Ops:
  0.6 45.1 %copy-start.2 = (s32[1,1,8,5]{2,1,3,0:T(1,128)S(1)}, s32[1,1,8,5]{2,1,3,0:T(1,128)}, u32[]{:S(2)}) copy-start(s32[1,1,8,5]{2,1,3,0:T(1,128)} %param.10) | copy-start | bytes 484
  0.6 45.1 %copy-start.3 = (s32[1,1,8,5]{2,1,3,0:T(1,128)S(1)}, s32[1,1,8,5]{2,1,3,0:T(1,128)}, u32[]{:S(2)}) copy-start(s32[1,1,8,5]{2,1,3,0:T(1,128)} %param.11) | copy-start | bytes 484
  0.7 45.1 %copy-start.5 = (s32[1,1,8]{2,1,0:T(1,128)S(1)}, s32[1,1,8]{2,1,0:T(1,128)}, u32[]{:S(2)}) copy-start(s32[1,1,8]{2,1,0:T(1,128)} %param.12) | copy-start | bytes 100
  10.4 35.3 %copy-start = (bf16[8,5,128,128]{3,2,1,0:T(8,128)(2,1)S(1)}, bf16[8,5,128,128]{3,2,1,0:T(8,128)(2,1)}, u32[]{:S(2)}) copy-start(bf16[8,5,128,128]{3,2,1,0:T(8,128)(2,1)} %get-tuple-element.18.schur) | copy-start | bytes 3932164
  10.4 7.4 %collective-permute-start = (bf16[1040,128]{1,0:T(8,128)(2,1)}, bf16[1040,128]{1,0:T(8,128)(2,1)S(1)}, u32[]{:S(2)}, u32[]{:S(2)}) collective-permute-start(bf16[1040,128]{1,0:T(8,128)(2,1)} %get-tuple-element.13), channel_id=1, source_target_pairs={{0,4},{4,0},{8,12},{12,8},{16,20},{20,16},{24,28},{28,24},{1,5},{5... | collective-permute-start | bytes 798728 | tf_op jit(solution)/shard_map/ppermute | solution.py:33
  10.9 11.2 %collective-permute-start.1 = (bf16[1040,128]{1,0:T(8,128)(2,1)}, bf16[1040,128]{1,0:T(8,128)(2,1)S(1)}, u32[]{:S(2)}, u32[]{:S(2)}) collective-permute-start(bf16[1040,128]{1,0:T(8,128)(2,1)} %get-tuple-element.14), channel_id=1, source_target_pairs={{0,28},{4,8},{8,4},{12,16},{16,12},{20,24},{24,20},{28,0},{1,29},{... | collective-permute-start | bytes 798728 | tf_op jit(solution)/shard_map/ppermute | solution.py:31
  15.7 8.3 %collective-permute-start.2 = (bf16[1040,128]{1,0:T(8,128)(2,1)}, bf16[1040,128]{1,0:T(8,128)(2,1)S(1)}, u32[]{:S(2)}, u32[]{:S(2)}) collective-permute-start(bf16[1040,128]{1,0:T(8,128)(2,1)} %get-tuple-element.15), channel_id=1, source_target_pairs={{0,1},{1,0},{2,3},{3,2},{4,5},{5,4},{6,7},{7,6},{8,9},{9,8},{10,11... | collective-permute-start | bytes 798728 | tf_op jit(solution)/shard_map/ppermute | solution.py:30
  17.1 6.8 %collective-permute-start.3 = (bf16[1040,128]{1,0:T(8,128)(2,1)}, bf16[1040,128]{1,0:T(8,128)(2,1)S(1)}, u32[]{:S(2)}, u32[]{:S(2)}) collective-permute-start(bf16[1040,128]{1,0:T(8,128)(2,1)} %get-tuple-element.16), channel_id=1, source_target_pairs={{1,2},{2,1},{5,6},{6,5},{9,10},{10,9},{13,14},{14,13},{17,18},{18,... | collective-permute-start | bytes 798728 | tf_op jit(solution)/shard_map/ppermute | solution.py:32
  24.0 1.0 %copy-start.1 = (f32[1024,128]{1,0:T(8,128)S(1)}, f32[1024,128]{1,0:T(8,128)}, u32[]{:S(2)}) copy-start(f32[1024,128]{1,0:T(8,128)} %get-tuple-element.11.own) | copy-start | bytes 1572868
  25.0 0.7 %copy-start.4 = (f32[16,128]{1,0:T(8,128)S(1)}, f32[16,128]{1,0:T(8,128)}, u32[]{:S(2)}) copy-start(f32[16,128]{1,0:T(8,128)} %get-tuple-element.12.own_cnt) | copy-start | bytes 24580
  26.7 9.6 %collective-permute-start.7 = (bf16[1024,128]{1,0:T(8,128)(2,1)S(1)}, bf16[1024,128]{1,0:T(8,128)(2,1)S(1)}, u32[]{:S(2)}, u32[]{:S(2)}) collective-permute-start(bf16[1024,128]{1,0:T(8,128)(2,1)S(1)} %get-tuple-element.19.avg), channel_id=1, source_target_pairs={{1,2},{2,1},{5,6},{6,5},{9,10},{10,9},{13,14},{14,13},{17,18},{18,... | collective-permute-start | bytes 786440 | tf_op jit(solution)/shard_map/ppermute | solution.py:32
  27.4 18.4 %collective-permute-start.6 = (bf16[1024,128]{1,0:T(8,128)(2,1)S(1)}, bf16[1024,128]{1,0:T(8,128)(2,1)S(1)}, u32[]{:S(2)}, u32[]{:S(2)}) collective-permute-start(bf16[1024,128]{1,0:T(8,128)(2,1)S(1)} %get-tuple-element.19.avg), channel_id=1, source_target_pairs={{0,1},{1,0},{2,3},{3,2},{4,5},{5,4},{6,7},{7,6},{8,9},{9,8},{10,11... | collective-permute-start | bytes 786440 | tf_op jit(solution)/shard_map/ppermute | solution.py:30
  35.6 10.1 %collective-permute-start.5 = (bf16[1024,128]{1,0:T(8,128)(2,1)S(1)}, bf16[1024,128]{1,0:T(8,128)(2,1)S(1)}, u32[]{:S(2)}, u32[]{:S(2)}) collective-permute-start(bf16[1024,128]{1,0:T(8,128)(2,1)S(1)} %get-tuple-element.19.avg), channel_id=1, source_target_pairs={{0,28},{4,8},{8,4},{12,16},{16,12},{20,24},{24,20},{28,0},{1,29},{... | collective-permute-start | bytes 786440 | tf_op jit(solution)/shard_map/ppermute | solution.py:31
  36.0 9.7 %collective-permute-start.4 = (bf16[1024,128]{1,0:T(8,128)(2,1)S(1)}, bf16[1024,128]{1,0:T(8,128)(2,1)S(1)}, u32[]{:S(2)}, u32[]{:S(2)}) collective-permute-start(bf16[1024,128]{1,0:T(8,128)(2,1)S(1)} %get-tuple-element.19.avg), channel_id=1, source_target_pairs={{0,4},{4,0},{8,12},{12,8},{16,20},{20,16},{24,28},{28,24},{1,5},{5... | collective-permute-start | bytes 786440 | tf_op jit(solution)/shard_map/ppermute | solution.py:33

commit v2 on v1

--- a/solution.py
+++ b/solution.py
@@ -8,6 +8,8 @@
 from jax.sharding import PartitionSpec as P
 
 PAD = 16
+SUMS_ORDER = ("near_a", "far_c", "far_a", "near_c")
+MEANS_ORDER = ("far_a", "far_c", "near_c", "near_a")
 
 
 def near_pairs(count):
@@ -25,13 +27,18 @@
     return pairs
 
 
-def swap_all(to_near_c, to_far_c, to_near_a, to_far_a):
+NAMES = ("near_c", "far_c", "near_a", "far_a")
+
+
+def swap_all(sent, order):
     circ, axial = lax.axis_size("circ"), lax.axis_size("axial")
-    near_a = lax.ppermute(to_near_a, "axial", near_pairs(axial))
-    far_c = lax.ppermute(to_far_c, "circ", far_pairs(circ, True))
-    far_a = lax.ppermute(to_far_a, "axial", far_pairs(axial, False))
-    near_c = lax.ppermute(to_near_c, "circ", near_pairs(circ))
-    return near_c, far_c, near_a, far_a
+    routes = {
+        "near_c": ("circ", near_pairs(circ)),
+        "far_c": ("circ", far_pairs(circ, True)),
+        "near_a": ("axial", near_pairs(axial)),
+        "far_a": ("axial", far_pairs(axial, False)),
+    }
+    return [lax.ppermute(sent[name], *routes[name]) for name in order]
 
 
 def buffer_of(code):
@@ -107,10 +114,13 @@
         avg_short[rows] = mean.astype(jnp.bfloat16)
 
 
-def deviation_kernel(dirs, slots, live, schur, avg, r1, r2, r3, r4, dev, table, stage, sems):
+def deviation_kernel(
+    order, dirs, slots, live, schur, avg, r1, r2, r3, r4, dev, table, stage, sems
+):
     subs, nblk, bs = schur.shape[0], schur.shape[1], schur.shape[2]
     own_slots = avg.shape[0] // bs
-    for b, r in enumerate((avg, r1, r2, r3, r4)):
+    places = [0] + [1 + NAMES.index(name) for name in order]
+    for b, r in zip(places, (avg, r1, r2, r3, r4)):
         for o in range(own_slots):
             table[b * own_slots + o] = r[o * bs:(o + 1) * bs]
     stores = []
@@ -131,23 +141,23 @@
     nblk, bs = diag.shape[1], diag.shape[2]
     own_slots = 8
     by_block = lambda x: jnp.transpose(x[0], (2, 0, 1))
-    dirs, slots, wts = by_block(directions), by_block(slot_ids), by_block(weights)
-    live = live_blocks[0]
+    in_hbm = lambda x: pltpu.with_memory_space_constraint(x, pltpu.HBM)
+    dirs, slots, wts = (in_hbm(by_block(x)) for x in (directions, slot_ids, weights))
+    live = in_hbm(live_blocks[0])
     f32, bf16 = jnp.float32, jnp.bfloat16
     rows = own_slots * bs
     smem = pl.BlockSpec(memory_space=pltpu.SMEM)
     vmem = pl.BlockSpec(memory_space=pltpu.VMEM)
     hbm = pl.BlockSpec(memory_space=pltpu.HBM)
-    sent = jax.ShapeDtypeStruct((rows + PAD, bs), bf16)
     schur, own, own_cnt, s1, s2, s3, s4 = pl.pallas_call(
         schur_kernel,
         in_specs=[smem] * 4 + [hbm] * 3,
         out_specs=[vmem] * 7,
         out_shape=[
-            jax.ShapeDtypeStruct((subs, nblk, bs, bs), bf16),
-            jax.ShapeDtypeStruct((rows, bs), f32),
-            jax.ShapeDtypeStruct((PAD, bs), f32),
-        ] + [sent] * 4,
+            pltpu.VMEM((subs, nblk, bs, bs), bf16),
+            pltpu.VMEM((rows, bs), f32),
+            pltpu.VMEM((PAD, bs), f32),
+        ] + [pltpu.VMEM((rows + PAD, bs), bf16)] * 4,
         scratch_shapes=[
             pltpu.VMEM(inv.shape, bf16),
             pltpu.VMEM(coup.shape, bf16),
@@ -158,8 +168,8 @@
         ],
         compiler_params=pltpu.CompilerParams(vmem_limit_bytes=56 * 2**20),
         name="schur_and_sums",
-    )(dirs, slots, live, wts, inv, coup, diag)
-    r1, r2, r3, r4 = swap_all(s1, s2, s3, s4)
+    )(dirs, slots, live, wts, in_hbm(inv), in_hbm(coup), in_hbm(diag))
+    received = swap_all(dict(zip(NAMES, (s1, s2, s3, s4))), SUMS_ORDER)
     avg, avg_short = pl.pallas_call(
         average_kernel,
         in_specs=[vmem] * 6,
@@ -170,10 +180,10 @@
         ],
         compiler_params=pltpu.CompilerParams(vmem_limit_bytes=16 * 2**20),
         name="average",
-    )(own, own_cnt, r1, r2, r3, r4)
-    n1, n2, n3, n4 = swap_all(avg_short, avg_short, avg_short, avg_short)
+    )(own, own_cnt, *received)
+    fetched = swap_all(dict.fromkeys(NAMES, avg_short), MEANS_ORDER)
     dev = pl.pallas_call(
-        deviation_kernel,
+        functools.partial(deviation_kernel, MEANS_ORDER),
         in_specs=[smem] * 3 + [vmem] * 6,
         out_specs=hbm,
         out_shape=jax.ShapeDtypeStruct((subs, nblk, bs, bs), bf16),
@@ -184,7 +194,7 @@
         ],
         compiler_params=pltpu.CompilerParams(vmem_limit_bytes=16 * 2**20),
         name="deviation",
-    )(dirs, slots, live, schur, avg_short, n1, n2, n3, n4)
+    )(dirs, slots, live, schur, avg_short, *fetched)
     return avg.reshape(1, 1, own_slots, bs, bs), dev[None, None]
 
 

time: 47.9 us -> 39.7 us (0.83)
  waiting for transfers between devices: 15.6 us -> 12.2 us
  local copies, waits for them, and re-layouts: 1.76 us -> 0 us
  Pallas kernels: 12.6 us -> 11.1 us
  starting transfers between devices: 16.9 us -> 15.4 us
    ppermute x8, waiting for transfers between devices: 15.6 us -> 12.2 us  [swap_all(): return [lax.ppermute(sent[name], *routes[name]) for name in order]]
    unnamed x12 -> x0, local copies, waits for them, and re-layouts: 1.76 us -> none
    pallas_call x1, Pallas kernels: 9.75 us -> 8.18 us  [body(): pl.pallas_call(schur_kernel, in_specs=[smem] * 4 + [hbm] * 3, out_specs=[...]
    ppermute x8, starting transfers between devices: 16.9 us -> 15.4 us  [swap_all(): return [lax.ppermute(sent[name], *routes[name]) for name in order]]
  transfers between devices with their start and end apart: 8 -> 8, of which waited for: 3 -> 4; matrix products, arithmetic and copies ran while one was open for 0% -> 0% of each run, Pallas kernels for 0% -> 0%
where the time goes in v2:
time: 39.7 us; the launch traced here: 39.5 us
  starting transfers between devices  15.4 us (39%)
  waiting for transfers between devices  12.2 us (31%)
  Pallas kernels  11.1 us (28%)
  between operations  0.67 us (2%)
    ppermute x8, starting transfers between devices, swap_all(): return [lax.ppermute(sent[name], *routes[name]) for name in order]  15.4 us
    ppermute x8, waiting for transfers between devices, swap_all(): return [lax.ppermute(sent[name], *routes[name]) for name in order]  12.2 us
    pallas_call x1, Pallas kernels, body(): pl.pallas_call(schur_kernel, in_specs=[smem] * 4 + [hbm] * 3, out_specs=[...  8.18 us
    pallas_call x1, Pallas kernels, body(): pl.pallas_call(functools.partial(deviation_kernel, MEANS_ORDER), in_specs...  2 us
    pallas_call x1, Pallas kernels, body(): pl.pallas_call(average_kernel, in_specs=[vmem] * 6, out_specs=[vmem] * 2,...  0.97 us
  transfers between devices with their start and end apart: 8, of which 4 were waited for; matrix products, arithmetic and copies ran while one was open for 0% of the time, Pallas kernels for 0%

profile of v2, /device:TPU:0, one launch (start us, length us, event | category | flops | bytes accessed | tf_op | source)
XLA Modules:
  0.0 39.5 jit_solution(9825996771152567561)
XLA Ops:
  0.6 8.2 %schur_and_sums.1 = (bf16[8,5,128,128]{3,2,1,0:T(8,128)(2,1)S(1)}, f32[1024,128]{1,0:T(8,128)S(1)}, f32[16,128]{1,0:T(8,128)S(1)}, bf16[1040,128]{1,0:T(8,128)(2...) custom-call(s32[5,1,8]{2,1,0:T(1,128)} %bitcast.19, ...), custom_call_target="tpu_custom_call" | custom-call | tf_op jit(solution)/shard_map/schur_and_sums/pallas_call | solution.py:152
  8.8 3.0 %collective-permute-start = (bf16[1040,128]{1,0:T(8,128)(2,1)S(1)}, bf16[1040,128]{1,0:T(8,128)(2,1)S(1)}, u32[]{:S(2)}, u32[]{:S(2)}) collective-permute-start(bf16[1040,128]{1,0:T(8,128)(2,1)S(1)} %get-tuple-element.13), channel_id=1, source_target_pairs={{0,1},{1,0},{2,3},{3,2},{4,5},{5,4},{6,7},{7,6},{8,9},{9,8},{10,11... | collective-permute-start | bytes 798728 | tf_op jit(solution)/shard_map/ppermute | solution.py:41
  11.8 2.8 %collective-permute-start.1 = (bf16[1040,128]{1,0:T(8,128)(2,1)S(1)}, bf16[1040,128]{1,0:T(8,128)(2,1)S(1)}, u32[]{:S(2)}, u32[]{:S(2)}) collective-permute-start(bf16[1040,128]{1,0:T(8,128)(2,1)S(1)} %get-tuple-element.14), channel_id=1, source_target_pairs={{0,28},{4,8},{8,4},{12,16},{16,12},{20,24},{24,20},{28,0},{1,29},{... | collective-permute-start | bytes 798728 | tf_op jit(solution)/shard_map/ppermute | solution.py:41
  14.6 0.7 %collective-permute-start.2 = (bf16[1040,128]{1,0:T(8,128)(2,1)S(1)}, bf16[1040,128]{1,0:T(8,128)(2,1)S(1)}, u32[]{:S(2)}, u32[]{:S(2)}) collective-permute-start(bf16[1040,128]{1,0:T(8,128)(2,1)S(1)} %get-tuple-element.15), channel_id=1, source_target_pairs={{1,2},{2,1},{5,6},{6,5},{9,10},{10,9},{13,14},{14,13},{17,18},{18,... | collective-permute-start | bytes 798728 | tf_op jit(solution)/shard_map/ppermute | solution.py:41
  15.2 0.1 collective-permute-start.3
  15.3 2.9 %collective-permute-done.r1 = bf16[1040,128]{1,0:T(8,128)(2,1)S(1)} collective-permute-done((bf16[1040,128]{1,0:T(8,128)(2,1)S(1)}, bf16[1040,128]{1,0:T(8,128)(2,1)S(1)}, u32[]{:S(2)}, u32[]{:S(2)}) %collective-permute-start) | collective-permute-done | bytes 266272 | tf_op jit(solution)/shard_map/ppermute | solution.py:41
  18.2 3.8 %collective-permute-done.1.r2 = bf16[1040,128]{1,0:T(8,128)(2,1)S(1)} collective-permute-done((bf16[1040,128]{1,0:T(8,128)(2,1)S(1)}, bf16[1040,128]{1,0:T(8,128)(2,1)S(1)}, u32[]{:S(2)}, u32[]{:S(2)}) %collective-permute-start.1) | collective-permute-done | bytes 266272 | tf_op jit(solution)/shard_map/ppermute | solution.py:41
  22.1 0.0 collective-permute-done.2.r3
  22.1 0.0 collective-permute-done.3.r4
  22.1 1.0 %average.1 = (f32[1024,128]{1,0:T(8,128)}, bf16[1024,128]{1,0:T(8,128)(2,1)S(1)}) custom-call(f32[1024,128]{1,0:T(8,128)S(1)} %get-tuple-element.11.own, f32[16,128]{1,0:T(8,128)S(1)} %get-tuple-element.12.own_cnt, bf16[1040,128]{1,0:T(8,128)(2,1)S(1)} %collective-permute-done.r1, bf16[1040,128]{1,0:T(8,128)(2,1)S(1)} %collective-permute-done.1.r2, ...), custom_call_target="tpu_custom_call" | custom-call | tf_op jit(solution)/shard_map/average/pallas_call | solution.py:173
  23.0 4.5 %collective-permute-start.7 = (bf16[1024,128]{1,0:T(8,128)(2,1)S(1)}, bf16[1024,128]{1,0:T(8,128)(2,1)S(1)}, u32[]{:S(2)}, u32[]{:S(2)}) collective-permute-start(bf16[1024,128]{1,0:T(8,128)(2,1)S(1)} %get-tuple-element.19.avg), channel_id=1, source_target_pairs={{0,1},{1,0},{2,3},{3,2},{4,5},{5,4},{6,7},{7,6},{8,9},{9,8},{10,11... | collective-permute-start | bytes 786440 | tf_op jit(solution)/shard_map/ppermute | solution.py:41
  27.6 0.0 collective-permute-start.6
  27.6 3.7 %collective-permute-start.5 = (bf16[1024,128]{1,0:T(8,128)(2,1)S(1)}, bf16[1024,128]{1,0:T(8,128)(2,1)S(1)}, u32[]{:S(2)}, u32[]{:S(2)}) collective-permute-start(bf16[1024,128]{1,0:T(8,128)(2,1)S(1)} %get-tuple-element.19.avg), channel_id=1, source_target_pairs={{0,28},{4,8},{8,4},{12,16},{16,12},{20,24},{24,20},{28,0},{1,29},{... | collective-permute-start | bytes 786440 | tf_op jit(solution)/shard_map/ppermute | solution.py:41
  31.3 0.7 %collective-permute-start.4 = (bf16[1024,128]{1,0:T(8,128)(2,1)S(1)}, bf16[1024,128]{1,0:T(8,128)(2,1)S(1)}, u32[]{:S(2)}, u32[]{:S(2)}) collective-permute-start(bf16[1024,128]{1,0:T(8,128)(2,1)S(1)} %get-tuple-element.19.avg), channel_id=1, source_target_pairs={{1,2},{2,1},{5,6},{6,5},{9,10},{10,9},{13,14},{14,13},{17,18},{18,... | collective-permute-start | bytes 786440 | tf_op jit(solution)/shard_map/ppermute | solution.py:41
  32.0 1.9 %collective-permute-done.7.r4 = bf16[1024,128]{1,0:T(8,128)(2,1)S(1)} collective-permute-done((bf16[1024,128]{1,0:T(8,128)(2,1)S(1)}, bf16[1024,128]{1,0:T(8,128)(2,1)S(1)}, u32[]{:S(2)}, u32[]{:S(2)}) %collective-permute-start.7) | collective-permute-done | bytes 262176 | tf_op jit(solution)/shard_map/ppermute | solution.py:41
  33.9 0.0 collective-permute-done.6.r3
  33.9 3.5 %collective-permute-done.5.r2 = bf16[1024,128]{1,0:T(8,128)(2,1)S(1)} collective-permute-done((bf16[1024,128]{1,0:T(8,128)(2,1)S(1)}, bf16[1024,128]{1,0:T(8,128)(2,1)S(1)}, u32[]{:S(2)}, u32[]{:S(2)}) %collective-permute-start.5) | collective-permute-done | bytes 262176 | tf_op jit(solution)/shard_map/ppermute | solution.py:41
  37.5 0.0 collective-permute-done.4.r1
  37.5 2.0 %deviation.1 = bf16[8,5,128,128]{3,2,1,0:T(8,128)(2,1)} custom-call(s32[5,1,8]{2,1,0:T(1,128)} %bitcast.20, s32[5,1,8]{2,1,0:T(1,128)} %bitcast.22, s32[1,8]{1,0:T(1,128)} %bitcast.25, bf16[8,5,128,128]{3,2,1,0:T(8,128)(2,1)S(1)} %get-tuple-element.18.schur, bf16[1024,128]{1,0:T(8,128)(2,1)S(1)} %get-tuple-element.19.avg, ...), custom_call_target="tpu_custom_call" | custom-call | tf_op jit(solution)/shard_map/deviation/pallas_call | solution.py:185
Async XLA Ops:
  8.8 9.4 %collective-permute-start = (bf16[1040,128]{1,0:T(8,128)(2,1)S(1)}, bf16[1040,128]{1,0:T(8,128)(2,1)S(1)}, u32[]{:S(2)}, u32[]{:S(2)}) collective-permute-start(bf16[1040,128]{1,0:T(8,128)(2,1)S(1)} %get-tuple-element.13), channel_id=1, source_target_pairs={{0,1},{1,0},{2,3},{3,2},{4,5},{5,4},{6,7},{7,6},{8,9},{9,8},{10,11... | collective-permute-start | bytes 798728 | tf_op jit(solution)/shard_map/ppermute | solution.py:41
  11.8 10.2 %collective-permute-start.1 = (bf16[1040,128]{1,0:T(8,128)(2,1)S(1)}, bf16[1040,128]{1,0:T(8,128)(2,1)S(1)}, u32[]{:S(2)}, u32[]{:S(2)}) collective-permute-start(bf16[1040,128]{1,0:T(8,128)(2,1)S(1)} %get-tuple-element.14), channel_id=1, source_target_pairs={{0,28},{4,8},{8,4},{12,16},{16,12},{20,24},{24,20},{28,0},{1,29},{... | collective-permute-start | bytes 798728 | tf_op jit(solution)/shard_map/ppermute | solution.py:41
  14.6 7.5 %collective-permute-start.2 = (bf16[1040,128]{1,0:T(8,128)(2,1)S(1)}, bf16[1040,128]{1,0:T(8,128)(2,1)S(1)}, u32[]{:S(2)}, u32[]{:S(2)}) collective-permute-start(bf16[1040,128]{1,0:T(8,128)(2,1)S(1)} %get-tuple-element.15), channel_id=1, source_target_pairs={{1,2},{2,1},{5,6},{6,5},{9,10},{10,9},{13,14},{14,13},{17,18},{18,... | collective-permute-start | bytes 798728 | tf_op jit(solution)/shard_map/ppermute | solution.py:41
  15.2 6.8 %collective-permute-start.3 = (bf16[1040,128]{1,0:T(8,128)(2,1)S(1)}, bf16[1040,128]{1,0:T(8,128)(2,1)S(1)}, u32[]{:S(2)}, u32[]{:S(2)}) collective-permute-start(bf16[1040,128]{1,0:T(8,128)(2,1)S(1)} %get-tuple-element.16), channel_id=1, source_target_pairs={{0,4},{4,0},{8,12},{12,8},{16,20},{20,16},{24,28},{28,24},{1,5},{5... | collective-permute-start | bytes 798728 | tf_op jit(solution)/shard_map/ppermute | solution.py:41
  23.0 10.9 %collective-permute-start.7 = (bf16[1024,128]{1,0:T(8,128)(2,1)S(1)}, bf16[1024,128]{1,0:T(8,128)(2,1)S(1)}, u32[]{:S(2)}, u32[]{:S(2)}) collective-permute-start(bf16[1024,128]{1,0:T(8,128)(2,1)S(1)} %get-tuple-element.19.avg), channel_id=1, source_target_pairs={{0,1},{1,0},{2,3},{3,2},{4,5},{5,4},{6,7},{7,6},{8,9},{9,8},{10,11... | collective-permute-start | bytes 786440 | tf_op jit(solution)/shard_map/ppermute | solution.py:41
  27.6 6.3 %collective-permute-start.6 = (bf16[1024,128]{1,0:T(8,128)(2,1)S(1)}, bf16[1024,128]{1,0:T(8,128)(2,1)S(1)}, u32[]{:S(2)}, u32[]{:S(2)}) collective-permute-start(bf16[1024,128]{1,0:T(8,128)(2,1)S(1)} %get-tuple-element.19.avg), channel_id=1, source_target_pairs={{0,4},{4,0},{8,12},{12,8},{16,20},{20,16},{24,28},{28,24},{1,5},{5... | collective-permute-start | bytes 786440 | tf_op jit(solution)/shard_map/ppermute | solution.py:41
  27.6 9.9 %collective-permute-start.5 = (bf16[1024,128]{1,0:T(8,128)(2,1)S(1)}, bf16[1024,128]{1,0:T(8,128)(2,1)S(1)}, u32[]{:S(2)}, u32[]{:S(2)}) collective-permute-start(bf16[1024,128]{1,0:T(8,128)(2,1)S(1)} %get-tuple-element.19.avg), channel_id=1, source_target_pairs={{0,28},{4,8},{8,4},{12,16},{16,12},{20,24},{24,20},{28,0},{1,29},{... | collective-permute-start | bytes 786440 | tf_op jit(solution)/shard_map/ppermute | solution.py:41
  31.3 6.2 %collective-permute-start.4 = (bf16[1024,128]{1,0:T(8,128)(2,1)S(1)}, bf16[1024,128]{1,0:T(8,128)(2,1)S(1)}, u32[]{:S(2)}, u32[]{:S(2)}) collective-permute-start(bf16[1024,128]{1,0:T(8,128)(2,1)S(1)} %get-tuple-element.19.avg), channel_id=1, source_target_pairs={{1,2},{2,1},{5,6},{6,5},{9,10},{10,9},{13,14},{14,13},{17,18},{18,... | collective-permute-start | bytes 786440 | tf_op jit(solution)/shard_map/ppermute | solution.py:41

commit v3 on v2

--- a/solution.py
+++ b/solution.py
@@ -38,6 +38,13 @@
         "near_a": ("axial", near_pairs(axial)),
         "far_a": ("axial", far_pairs(axial, False)),
     }
+    diagonal = []
+    for row in range(circ):
+        for i, j in far_pairs(axial, False):
+            diagonal.append((row * axial + i, row * axial + j))
+        for i in (0, axial - 1):
+            diagonal.append((row * axial + i, (row ^ 1) * axial + i))
+    routes["far_a"] = (("circ", "axial"), diagonal)
     return [lax.ppermute(sent[name], *routes[name]) for name in order]
 
 
@@ -49,10 +56,19 @@
     return jnp.where(code == 0, 0, jnp.where(code <= 2, circ, axial))
 
 
+def load_tables(sources, tables, sems):
+    copies = [
+        pltpu.make_async_copy(a, b, sems.at[j]) for j, (a, b) in enumerate(zip(sources, tables))
+    ]
+    for copy in copies:
+        copy.start()
+    return copies
+
+
 def schur_kernel(
-    dirs, slots, live, weights, inv, coup, diag,
+    dirs_h, slots_h, live_h, weights_h, inv, coup, diag,
     schur, own, own_cnt, s1, s2, s3, s4,
-    inv_v, coup_v, diag_v, acc, cnt, sems,
+    dirs, slots, live, weights, inv_v, coup_v, diag_v, acc, cnt, sems, table_sems,
 ):
     subs, nblk, bs = diag.shape[0], diag.shape[1], diag.shape[2]
     own_slots = own.shape[0] // bs
@@ -64,26 +80,37 @@
             for j, (a, b) in enumerate(pairs)
         ]
 
-    for sub in range(subs):
+    for copy in loads(0):
+        copy.start()
+    tables = load_tables(
+        (dirs_h, slots_h, live_h, weights_h), (dirs, slots, live, weights), table_sems
+    )
+    for sub in range(1, subs):
         for copy in loads(sub):
             copy.start()
     acc[...] = jnp.zeros_like(acc)
     cnt[...] = jnp.zeros_like(cnt)
-
-    def step(sub, carry):
-        for copy in loads(sub):
-            copy.wait()
-        c = coup_v[sub]
+    for copy in tables:
+        copy.wait()
+
+    def blocks(sub, count):
+        c = coup_v[sub, :, :count * bs]
         st = jnp.dot(c.T, inv_v[sub], preferred_element_type=jnp.float32).astype(jnp.bfloat16)
-        for k in range(nblk):
+        for k in range(count):
             cols = slice(k * bs, (k + 1) * bs)
             trail = jnp.dot(st[cols], c[:, cols], preferred_element_type=jnp.float32)
             block = (diag_v[sub, k].astype(jnp.float32) - trail).astype(jnp.bfloat16)
             schur[sub, k] = block
-            w = jnp.where(k < live[0, sub], weights[k, 0, sub], 0).astype(jnp.float32)
+            w = weights[k, 0, sub].astype(jnp.float32)
             buf, slot = buffer_of(dirs[k, 0, sub]), slots[k, 0, sub]
             acc[buf * own_slots + slot] += w * block.astype(jnp.float32)
             cnt[buf, pl.ds(slot, 1), :] += jnp.full((1, bs), w, jnp.float32)
+
+    def step(sub, carry):
+        for copy in loads(sub):
+            copy.wait()
+        for count in range(1, nblk + 1):
+            pl.when(live[0, sub] == count)(functools.partial(blocks, sub, count))
         return carry
 
     lax.fori_loop(0, subs, step, 0)
@@ -115,14 +142,18 @@
 
 
 def deviation_kernel(
-    order, dirs, slots, live, schur, avg, r1, r2, r3, r4, dev, table, stage, sems
+    order, dirs_h, slots_h, live_h, schur, avg, r1, r2, r3, r4, dev,
+    dirs, slots, live, table, stage, sems, table_sems,
 ):
+    tables = load_tables((dirs_h, slots_h, live_h), (dirs, slots, live), table_sems)
     subs, nblk, bs = schur.shape[0], schur.shape[1], schur.shape[2]
     own_slots = avg.shape[0] // bs
     places = [0] + [1 + NAMES.index(name) for name in order]
     for b, r in zip(places, (avg, r1, r2, r3, r4)):
         for o in range(own_slots):
             table[b * own_slots + o] = r[o * bs:(o + 1) * bs]
+    for copy in tables:
+        copy.wait()
     stores = []
     for s in range(subs):
         for k in range(nblk):
@@ -146,12 +177,11 @@
     live = in_hbm(live_blocks[0])
     f32, bf16 = jnp.float32, jnp.bfloat16
     rows = own_slots * bs
-    smem = pl.BlockSpec(memory_space=pltpu.SMEM)
     vmem = pl.BlockSpec(memory_space=pltpu.VMEM)
     hbm = pl.BlockSpec(memory_space=pltpu.HBM)
     schur, own, own_cnt, s1, s2, s3, s4 = pl.pallas_call(
         schur_kernel,
-        in_specs=[smem] * 4 + [hbm] * 3,
+        in_specs=[hbm] * 7,
         out_specs=[vmem] * 7,
         out_shape=[
             pltpu.VMEM((subs, nblk, bs, bs), bf16),
@@ -159,12 +189,17 @@
             pltpu.VMEM((PAD, bs), f32),
         ] + [pltpu.VMEM((rows + PAD, bs), bf16)] * 4,
         scratch_shapes=[
+            pltpu.SMEM(dirs.shape, jnp.int32),
+            pltpu.SMEM(slots.shape, jnp.int32),
+            pltpu.SMEM(live.shape, jnp.int32),
+            pltpu.SMEM(wts.shape, jnp.int32),
             pltpu.VMEM(inv.shape, bf16),
             pltpu.VMEM(coup.shape, bf16),
             pltpu.VMEM(diag.shape, bf16),
             pltpu.VMEM((5 * own_slots, bs, bs), f32),
             pltpu.VMEM((5, PAD, bs), f32),
             pltpu.SemaphoreType.DMA((3, subs)),
+            pltpu.SemaphoreType.DMA((4,)),
         ],
         compiler_params=pltpu.CompilerParams(vmem_limit_bytes=56 * 2**20),
         name="schur_and_sums",
@@ -184,13 +219,17 @@
     fetched = swap_all(dict.fromkeys(NAMES, avg_short), MEANS_ORDER)
     dev = pl.pallas_call(
         functools.partial(deviation_kernel, MEANS_ORDER),
-        in_specs=[smem] * 3 + [vmem] * 6,
+        in_specs=[hbm] * 3 + [vmem] * 6,
         out_specs=hbm,
         out_shape=jax.ShapeDtypeStruct((subs, nblk, bs, bs), bf16),
         scratch_shapes=[
+            pltpu.SMEM(dirs.shape, jnp.int32),
+            pltpu.SMEM(slots.shape, jnp.int32),
+            pltpu.SMEM(live.shape, jnp.int32),
             pltpu.VMEM((5 * own_slots, bs, bs), bf16),
             pltpu.VMEM((subs, nblk, bs, bs), bf16),
             pltpu.SemaphoreType.DMA((subs,)),
+            pltpu.SemaphoreType.DMA((3,)),
         ],
         compiler_params=pltpu.CompilerParams(vmem_limit_bytes=16 * 2**20),
         name="deviation",

time: 39.7 us -> 38.3 us (0.965)
  Pallas kernels: 11.1 us -> 9.62 us
  waiting for transfers between devices: 12.2 us -> 13.4 us
  starting transfers between devices: 15.4 us -> 14.7 us
    pallas_call x1, Pallas kernels: 8.18 us -> 6.69 us  [body(): pl.pallas_call(schur_kernel, in_specs=[hbm] * 7, out_specs=[vmem] * 7, ou...]
    ppermute x8, waiting for transfers between devices: 12.2 us -> 13.4 us  [swap_all(): return [lax.ppermute(sent[name], *routes[name]) for name in order]]
    ppermute x8, starting transfers between devices: 15.4 us -> 14.7 us  [swap_all(): return [lax.ppermute(sent[name], *routes[name]) for name in order]]
where the time goes in v3:
time: 38.3 us
  starting transfers between devices  14.7 us (38%)
  waiting for transfers between devices  13.4 us (35%)
  Pallas kernels  9.62 us (25%)
  between operations  0.65 us (2%)
    ppermute x8, starting transfers between devices, swap_all(): return [lax.ppermute(sent[name], *routes[name]) for name in order]  14.7 us
    ppermute x8, waiting for transfers between devices, swap_all(): return [lax.ppermute(sent[name], *routes[name]) for name in order]  13.4 us
    pallas_call x1, Pallas kernels, body(): pl.pallas_call(schur_kernel, in_specs=[hbm] * 7, out_specs=[vmem] * 7, ou...  6.69 us
    pallas_call x1, Pallas kernels, body(): pl.pallas_call(functools.partial(deviation_kernel, MEANS_ORDER), in_specs...  1.96 us
    pallas_call x1, Pallas kernels, body(): pl.pallas_call(average_kernel, in_specs=[vmem] * 6, out_specs=[vmem] * 2,...  0.97 us
  transfers between devices with their start and end apart: 8, of which 4 were waited for; matrix products, arithmetic and copies ran while one was open for 0% of the time, Pallas kernels for 0%

profile of v3, /device:TPU:0, one launch (start us, length us, event | category | flops | bytes accessed | tf_op | source)
XLA Modules:
  0.0 38.3 jit_solution(6115953949871480858)
XLA Ops:
  0.6 6.7 %schur_and_sums.1 = (bf16[8,5,128,128]{3,2,1,0:T(8,128)(2,1)S(1)}, f32[1024,128]{1,0:T(8,128)S(1)}, f32[16,128]{1,0:T(8,128)S(1)}, bf16[1040,128]{1,0:T(8,128)(2...) custom-call(s32[5,1,8]{2,1,0:T(1,128)} %bitcast.19, ...), custom_call_target="tpu_custom_call" | custom-call | tf_op jit(solution)/shard_map/schur_and_sums/pallas_call | solution.py:182
  7.3 2.8 %collective-permute-start = (bf16[1040,128]{1,0:T(8,128)(2,1)S(1)}, bf16[1040,128]{1,0:T(8,128)(2,1)S(1)}, u32[]{:S(2)}, u32[]{:S(2)}) collective-permute-start(bf16[1040,128]{1,0:T(8,128)(2,1)S(1)} %get-tuple-element.13), channel_id=1, source_target_pairs={{0,1},{1,0},{2,3},{3,2},{4,5},{5,4},{6,7},{7,6},{8,9},{9,8},{10,11... | collective-permute-start | bytes 798728 | tf_op jit(solution)/shard_map/ppermute | solution.py:48
  10.1 3.0 %collective-permute-start.1 = (bf16[1040,128]{1,0:T(8,128)(2,1)S(1)}, bf16[1040,128]{1,0:T(8,128)(2,1)S(1)}, u32[]{:S(2)}, u32[]{:S(2)}) collective-permute-start(bf16[1040,128]{1,0:T(8,128)(2,1)S(1)} %get-tuple-element.14), channel_id=1, source_target_pairs={{0,28},{4,8},{8,4},{12,16},{16,12},{20,24},{24,20},{28,0},{1,29},{... | collective-permute-start | bytes 798728 | tf_op jit(solution)/shard_map/ppermute | solution.py:48
  13.1 0.0 collective-permute-start.2
  13.1 0.5 %collective-permute-start.3 = (bf16[1040,128]{1,0:T(8,128)(2,1)S(1)}, bf16[1040,128]{1,0:T(8,128)(2,1)S(1)}, u32[]{:S(2)}, u32[]{:S(2)}) collective-permute-start(bf16[1040,128]{1,0:T(8,128)(2,1)S(1)} %get-tuple-element.16), channel_id=1, source_target_pairs={{0,4},{4,0},{8,12},{12,8},{16,20},{20,16},{24,28},{28,24},{1,5},{5... | collective-permute-start | bytes 798728 | tf_op jit(solution)/shard_map/ppermute | solution.py:48
  13.6 3.7 %collective-permute-done.r1 = bf16[1040,128]{1,0:T(8,128)(2,1)S(1)} collective-permute-done((bf16[1040,128]{1,0:T(8,128)(2,1)S(1)}, bf16[1040,128]{1,0:T(8,128)(2,1)S(1)}, u32[]{:S(2)}, u32[]{:S(2)}) %collective-permute-start) | collective-permute-done | bytes 266272 | tf_op jit(solution)/shard_map/ppermute | solution.py:48
  17.4 3.0 %collective-permute-done.1.r2 = bf16[1040,128]{1,0:T(8,128)(2,1)S(1)} collective-permute-done((bf16[1040,128]{1,0:T(8,128)(2,1)S(1)}, bf16[1040,128]{1,0:T(8,128)(2,1)S(1)}, u32[]{:S(2)}, u32[]{:S(2)}) %collective-permute-start.1) | collective-permute-done | bytes 266272 | tf_op jit(solution)/shard_map/ppermute | solution.py:48
  20.4 0.0 collective-permute-done.2.r3
  20.4 0.0 collective-permute-done.3.r4
  20.4 1.0 %average.1 = (f32[1024,128]{1,0:T(8,128)}, bf16[1024,128]{1,0:T(8,128)(2,1)S(1)}) custom-call(f32[1024,128]{1,0:T(8,128)S(1)} %get-tuple-element.11.own, f32[16,128]{1,0:T(8,128)S(1)} %get-tuple-element.12.own_cnt, bf16[1040,128]{1,0:T(8,128)(2,1)S(1)} %collective-permute-done.r1, bf16[1040,128]{1,0:T(8,128)(2,1)S(1)} %collective-permute-done.1.r2, ...), custom_call_target="tpu_custom_call" | custom-call | tf_op jit(solution)/shard_map/average/pallas_call | solution.py:208
  21.4 4.1 %collective-permute-start.7 = (bf16[1024,128]{1,0:T(8,128)(2,1)S(1)}, bf16[1024,128]{1,0:T(8,128)(2,1)S(1)}, u32[]{:S(2)}, u32[]{:S(2)}) collective-permute-start(bf16[1024,128]{1,0:T(8,128)(2,1)S(1)} %get-tuple-element.19.avg), channel_id=1, source_target_pairs={{0,1},{1,0},{2,3},{3,2},{4,5},{5,4},{6,7},{7,6},{8,9},{9,8},{10,11... | collective-permute-start | bytes 786440 | tf_op jit(solution)/shard_map/ppermute | solution.py:48
  25.5 0.0 collective-permute-start.6
  25.5 4.2 %collective-permute-start.5 = (bf16[1024,128]{1,0:T(8,128)(2,1)S(1)}, bf16[1024,128]{1,0:T(8,128)(2,1)S(1)}, u32[]{:S(2)}, u32[]{:S(2)}) collective-permute-start(bf16[1024,128]{1,0:T(8,128)(2,1)S(1)} %get-tuple-element.19.avg), channel_id=1, source_target_pairs={{0,28},{4,8},{8,4},{12,16},{16,12},{20,24},{24,20},{28,0},{1,29},{... | collective-permute-start | bytes 786440 | tf_op jit(solution)/shard_map/ppermute | solution.py:48
  29.7 0.0 collective-permute-start.4
  29.7 2.3 %collective-permute-done.7.r4 = bf16[1024,128]{1,0:T(8,128)(2,1)S(1)} collective-permute-done((bf16[1024,128]{1,0:T(8,128)(2,1)S(1)}, bf16[1024,128]{1,0:T(8,128)(2,1)S(1)}, u32[]{:S(2)}, u32[]{:S(2)}) %collective-permute-start.7) | collective-permute-done | bytes 262176 | tf_op jit(solution)/shard_map/ppermute | solution.py:48
  32.0 0.0 collective-permute-done.6.r3
  32.0 4.3 %collective-permute-done.5.r2 = bf16[1024,128]{1,0:T(8,128)(2,1)S(1)} collective-permute-done((bf16[1024,128]{1,0:T(8,128)(2,1)S(1)}, bf16[1024,128]{1,0:T(8,128)(2,1)S(1)}, u32[]{:S(2)}, u32[]{:S(2)}) %collective-permute-start.5) | collective-permute-done | bytes 262176 | tf_op jit(solution)/shard_map/ppermute | solution.py:48
  36.3 0.0 collective-permute-done.4.r1
  36.3 2.0 %deviation.1 = bf16[8,5,128,128]{3,2,1,0:T(8,128)(2,1)} custom-call(s32[5,1,8]{2,1,0:T(1,128)} %bitcast.20, s32[5,1,8]{2,1,0:T(1,128)} %bitcast.22, s32[1,8]{1,0:T(1,128)} %bitcast.25, bf16[8,5,128,128]{3,2,1,0:T(8,128)(2,1)S(1)} %get-tuple-element.18.schur, bf16[1024,128]{1,0:T(8,128)(2,1)S(1)} %get-tuple-element.19.avg, ...), custom_call_target="tpu_custom_call" | custom-call | tf_op jit(solution)/shard_map/deviation/pallas_call | solution.py:220
Async XLA Ops:
  7.3 10.0 %collective-permute-start = (bf16[1040,128]{1,0:T(8,128)(2,1)S(1)}, bf16[1040,128]{1,0:T(8,128)(2,1)S(1)}, u32[]{:S(2)}, u32[]{:S(2)}) collective-permute-start(bf16[1040,128]{1,0:T(8,128)(2,1)S(1)} %get-tuple-element.13), channel_id=1, source_target_pairs={{0,1},{1,0},{2,3},{3,2},{4,5},{5,4},{6,7},{7,6},{8,9},{9,8},{10,11... | collective-permute-start | bytes 798728 | tf_op jit(solution)/shard_map/ppermute | solution.py:48
  10.1 10.3 %collective-permute-start.1 = (bf16[1040,128]{1,0:T(8,128)(2,1)S(1)}, bf16[1040,128]{1,0:T(8,128)(2,1)S(1)}, u32[]{:S(2)}, u32[]{:S(2)}) collective-permute-start(bf16[1040,128]{1,0:T(8,128)(2,1)S(1)} %get-tuple-element.14), channel_id=1, source_target_pairs={{0,28},{4,8},{8,4},{12,16},{16,12},{20,24},{24,20},{28,0},{1,29},{... | collective-permute-start | bytes 798728 | tf_op jit(solution)/shard_map/ppermute | solution.py:48
  13.1 7.3 %collective-permute-start.2 = (bf16[1040,128]{1,0:T(8,128)(2,1)S(1)}, bf16[1040,128]{1,0:T(8,128)(2,1)S(1)}, u32[]{:S(2)}, u32[]{:S(2)}) collective-permute-start(bf16[1040,128]{1,0:T(8,128)(2,1)S(1)} %get-tuple-element.15), channel_id=1, source_target_pairs={{1,2},{2,1},{0,4},{3,7},{5,6},{6,5},{4,0},{7,3},{9,10},{10,9},{8,1... | collective-permute-start | bytes 798728 | tf_op jit(solution)/shard_map/ppermute | solution.py:48
  13.1 7.3 %collective-permute-start.3 = (bf16[1040,128]{1,0:T(8,128)(2,1)S(1)}, bf16[1040,128]{1,0:T(8,128)(2,1)S(1)}, u32[]{:S(2)}, u32[]{:S(2)}) collective-permute-start(bf16[1040,128]{1,0:T(8,128)(2,1)S(1)} %get-tuple-element.16), channel_id=1, source_target_pairs={{0,4},{4,0},{8,12},{12,8},{16,20},{20,16},{24,28},{28,24},{1,5},{5... | collective-permute-start | bytes 798728 | tf_op jit(solution)/shard_map/ppermute | solution.py:48
  21.4 10.7 %collective-permute-start.7 = (bf16[1024,128]{1,0:T(8,128)(2,1)S(1)}, bf16[1024,128]{1,0:T(8,128)(2,1)S(1)}, u32[]{:S(2)}, u32[]{:S(2)}) collective-permute-start(bf16[1024,128]{1,0:T(8,128)(2,1)S(1)} %get-tuple-element.19.avg), channel_id=1, source_target_pairs={{0,1},{1,0},{2,3},{3,2},{4,5},{5,4},{6,7},{7,6},{8,9},{9,8},{10,11... | collective-permute-start | bytes 786440 | tf_op jit(solution)/shard_map/ppermute | solution.py:48
  25.5 6.6 %collective-permute-start.6 = (bf16[1024,128]{1,0:T(8,128)(2,1)S(1)}, bf16[1024,128]{1,0:T(8,128)(2,1)S(1)}, u32[]{:S(2)}, u32[]{:S(2)}) collective-permute-start(bf16[1024,128]{1,0:T(8,128)(2,1)S(1)} %get-tuple-element.19.avg), channel_id=1, source_target_pairs={{0,4},{4,0},{8,12},{12,8},{16,20},{20,16},{24,28},{28,24},{1,5},{5... | collective-permute-start | bytes 786440 | tf_op jit(solution)/shard_map/ppermute | solution.py:48
  25.5 10.9 %collective-permute-start.5 = (bf16[1024,128]{1,0:T(8,128)(2,1)S(1)}, bf16[1024,128]{1,0:T(8,128)(2,1)S(1)}, u32[]{:S(2)}, u32[]{:S(2)}) collective-permute-start(bf16[1024,128]{1,0:T(8,128)(2,1)S(1)} %get-tuple-element.19.avg), channel_id=1, source_target_pairs={{0,28},{4,8},{8,4},{12,16},{16,12},{20,24},{24,20},{28,0},{1,29},{... | collective-permute-start | bytes 786440 | tf_op jit(solution)/shard_map/ppermute | solution.py:48
  29.7 6.6 %collective-permute-start.4 = (bf16[1024,128]{1,0:T(8,128)(2,1)S(1)}, bf16[1024,128]{1,0:T(8,128)(2,1)S(1)}, u32[]{:S(2)}, u32[]{:S(2)}) collective-permute-start(bf16[1024,128]{1,0:T(8,128)(2,1)S(1)} %get-tuple-element.19.avg), channel_id=1, source_target_pairs={{1,2},{2,1},{0,4},{3,7},{5,6},{6,5},{4,0},{7,3},{9,10},{10,9},{8,1... | collective-permute-start | bytes 786440 | tf_op jit(solution)/shard_map/ppermute | solution.py:48

commit v4 on v3

--- a/solution.py
+++ b/solution.py
@@ -67,7 +67,7 @@
 
 def schur_kernel(
     dirs_h, slots_h, live_h, weights_h, inv, coup, diag,
-    schur, own, own_cnt, s1, s2, s3, s4,
+    schur, own, own_cnt, s1, s2, s3, s4, places,
     dirs, slots, live, weights, inv_v, coup_v, diag_v, acc, cnt, sems, table_sems,
 ):
     subs, nblk, bs = diag.shape[0], diag.shape[1], diag.shape[2]
@@ -113,6 +113,10 @@
             pl.when(live[0, sub] == count)(functools.partial(blocks, sub, count))
         return carry
 
+    for sub in range(subs):
+        for k in range(nblk):
+            at = buffer_of(dirs[k, 0, sub]) * own_slots + slots[k, 0, sub]
+            places[k, sub] = jnp.where(k < live[0, sub], at, -1)
     lax.fori_loop(0, subs, step, 0)
     for o in range(own_slots):
         own[o * bs:(o + 1) * bs] = acc[o]
@@ -142,28 +146,27 @@
 
 
 def deviation_kernel(
-    order, dirs_h, slots_h, live_h, schur, avg, r1, r2, r3, r4, dev,
-    dirs, slots, live, table, stage, sems, table_sems,
+    order, at, schur, mean, avg, r1, r2, r3, r4, mean_out, dev, table, stage, sems, mean_sem
 ):
-    tables = load_tables((dirs_h, slots_h, live_h), (dirs, slots, live), table_sems)
+    mean_copy = pltpu.make_async_copy(mean, mean_out, mean_sem)
+    mean_copy.start()
     subs, nblk, bs = schur.shape[0], schur.shape[1], schur.shape[2]
     own_slots = avg.shape[0] // bs
-    places = [0] + [1 + NAMES.index(name) for name in order]
-    for b, r in zip(places, (avg, r1, r2, r3, r4)):
+    segments = [0] + [1 + NAMES.index(name) for name in order]
+    for b, r in zip(segments, (avg, r1, r2, r3, r4)):
         for o in range(own_slots):
             table[b * own_slots + o] = r[o * bs:(o + 1) * bs]
-    for copy in tables:
-        copy.wait()
     stores = []
     for s in range(subs):
         for k in range(nblk):
-            at = buffer_of(dirs[k, 0, s]) * own_slots + slots[k, 0, s]
-            diff = schur[s, k].astype(jnp.float32) - table[at].astype(jnp.float32)
-            stage[s, k] = jnp.where(k < live[0, s], diff, 0.0).astype(jnp.bfloat16)
+            place = at[k, s]
+            diff = schur[s, k] - table[jnp.maximum(place, 0)]
+            stage[s, k] = jnp.where(place >= 0, diff, jnp.zeros_like(diff))
         stores.append(pltpu.make_async_copy(stage.at[s], dev.at[s], sems.at[s]))
         stores[-1].start()
     for copy in stores:
         copy.wait()
+    mean_copy.wait()
 
 
 def body(interior_inv, coupling, boundary_diag, directions, slot_ids, live_blocks, weights):
@@ -179,15 +182,16 @@
     rows = own_slots * bs
     vmem = pl.BlockSpec(memory_space=pltpu.VMEM)
     hbm = pl.BlockSpec(memory_space=pltpu.HBM)
-    schur, own, own_cnt, s1, s2, s3, s4 = pl.pallas_call(
+    smem = pl.BlockSpec(memory_space=pltpu.SMEM)
+    schur, own, own_cnt, s1, s2, s3, s4, places = pl.pallas_call(
         schur_kernel,
         in_specs=[hbm] * 7,
-        out_specs=[vmem] * 7,
+        out_specs=[vmem] * 7 + [smem],
         out_shape=[
             pltpu.VMEM((subs, nblk, bs, bs), bf16),
             pltpu.VMEM((rows, bs), f32),
             pltpu.VMEM((PAD, bs), f32),
-        ] + [pltpu.VMEM((rows + PAD, bs), bf16)] * 4,
+        ] + [pltpu.VMEM((rows + PAD, bs), bf16)] * 4 + [pltpu.SMEM((nblk, subs), jnp.int32)],
         scratch_shapes=[
             pltpu.SMEM(dirs.shape, jnp.int32),
             pltpu.SMEM(slots.shape, jnp.int32),
@@ -210,31 +214,31 @@
         in_specs=[vmem] * 6,
         out_specs=[vmem] * 2,
         out_shape=[
-            jax.ShapeDtypeStruct((rows, bs), f32),
-            jax.ShapeDtypeStruct((rows, bs), bf16),
+            pltpu.VMEM((rows, bs), f32),
+            pltpu.VMEM((rows, bs), bf16),
         ],
         compiler_params=pltpu.CompilerParams(vmem_limit_bytes=16 * 2**20),
         name="average",
     )(own, own_cnt, *received)
     fetched = swap_all(dict.fromkeys(NAMES, avg_short), MEANS_ORDER)
-    dev = pl.pallas_call(
+    averaged, dev = pl.pallas_call(
         functools.partial(deviation_kernel, MEANS_ORDER),
-        in_specs=[hbm] * 3 + [vmem] * 6,
-        out_specs=hbm,
-        out_shape=jax.ShapeDtypeStruct((subs, nblk, bs, bs), bf16),
+        in_specs=[smem] + [vmem] * 7,
+        out_specs=[hbm] * 2,
+        out_shape=[
+            jax.ShapeDtypeStruct((rows, bs), f32),
+            jax.ShapeDtypeStruct((subs, nblk, bs, bs), bf16),
+        ],
         scratch_shapes=[
-            pltpu.SMEM(dirs.shape, jnp.int32),
-            pltpu.SMEM(slots.shape, jnp.int32),
-            pltpu.SMEM(live.shape, jnp.int32),
             pltpu.VMEM((5 * own_slots, bs, bs), bf16),
             pltpu.VMEM((subs, nblk, bs, bs), bf16),
             pltpu.SemaphoreType.DMA((subs,)),
-            pltpu.SemaphoreType.DMA((3,)),
+            pltpu.SemaphoreType.DMA,
         ],
         compiler_params=pltpu.CompilerParams(vmem_limit_bytes=16 * 2**20),
         name="deviation",
-    )(dirs, slots, live, schur, avg_short, *fetched)
-    return avg.reshape(1, 1, own_slots, bs, bs), dev[None, None]
+    )(pltpu.with_memory_space_constraint(places, pltpu.SMEM), schur, avg, avg_short, *fetched)
+    return averaged.reshape(1, 1, own_slots, bs, bs), dev[None, None]
 
 
 def solution(mesh):

time: 38.3 us -> 37 us (0.966); the launches traced: 38.3 us -> 36.6 us
  Pallas kernels: 9.62 us -> 8.22 us
  waiting for transfers between devices: 13.4 us -> 13 us
    pallas_call x1, Pallas kernels: 0.97 us -> 0.19 us  [body(): pl.pallas_call(average_kernel, in_specs=[vmem] * 6, out_specs=[vmem] * 2,...]
    pallas_call x1, Pallas kernels: 1.96 us -> 1.43 us  [body(): pl.pallas_call(functools.partial(deviation_kernel, MEANS_ORDER), in_specs...]
    ppermute x8, waiting for transfers between devices: 13.4 us -> 13 us  [swap_all(): return [lax.ppermute(sent[name], *routes[name]) for name in order]]
where the time goes in v4:
time: 37 us; the launch traced here: 36.6 us
  starting transfers between devices  14.7 us (40%)
  waiting for transfers between devices  13 us (35%)
  Pallas kernels  8.22 us (22%)
  between operations  0.65 us (2%)
    ppermute x8, starting transfers between devices, swap_all(): return [lax.ppermute(sent[name], *routes[name]) for name in order]  14.7 us
    ppermute x8, waiting for transfers between devices, swap_all(): return [lax.ppermute(sent[name], *routes[name]) for name in order]  13 us
    pallas_call x1, Pallas kernels, body(): pl.pallas_call(schur_kernel, in_specs=[hbm] * 7, out_specs=[vmem] * 7 + [...  6.59 us
    pallas_call x1, Pallas kernels, body(): pl.pallas_call(functools.partial(deviation_kernel, MEANS_ORDER), in_specs...  1.43 us
  transfers between devices with their start and end apart: 8, of which 4 were waited for; matrix products, arithmetic and copies ran while one was open for 0% of the time, Pallas kernels for 0%

profile of v4, /device:TPU:0, one launch (start us, length us, event | category | flops | bytes accessed | tf_op | source)
XLA Modules:
  0.0 36.6 jit_solution(7626187589403388627)
XLA Ops:
  0.6 6.6 %schur_and_sums.1 = (bf16[8,5,128,128]{3,2,1,0:T(8,128)(2,1)S(1)}, f32[1024,128]{1,0:T(8,128)S(1)}, f32[16,128]{1,0:T(8,128)S(1)}, bf16[1040,128]{1,0:T(8,128)(2...) custom-call(s32[5,1,8]{2,1,0:T(1,128)} %bitcast.18, ...), custom_call_target="tpu_custom_call" | custom-call | tf_op jit(solution)/shard_map/schur_and_sums/pallas_call | solution.py:186
  7.2 2.3 %collective-permute-start = (bf16[1040,128]{1,0:T(8,128)(2,1)S(1)}, bf16[1040,128]{1,0:T(8,128)(2,1)S(1)}, u32[]{:S(2)}, u32[]{:S(2)}) collective-permute-start(bf16[1040,128]{1,0:T(8,128)(2,1)S(1)} %get-tuple-element.18), channel_id=1, source_target_pairs={{0,1},{1,0},{2,3},{3,2},{4,5},{5,4},{6,7},{7,6},{8,9},{9,8},{10,11... | collective-permute-start | bytes 798728 | tf_op jit(solution)/shard_map/ppermute | solution.py:48
  9.5 2.9 %collective-permute-start.1 = (bf16[1040,128]{1,0:T(8,128)(2,1)S(1)}, bf16[1040,128]{1,0:T(8,128)(2,1)S(1)}, u32[]{:S(2)}, u32[]{:S(2)}) collective-permute-start(bf16[1040,128]{1,0:T(8,128)(2,1)S(1)} %get-tuple-element.19), channel_id=1, source_target_pairs={{0,28},{4,8},{8,4},{12,16},{16,12},{20,24},{24,20},{28,0},{1,29},{... | collective-permute-start | bytes 798728 | tf_op jit(solution)/shard_map/ppermute | solution.py:48
  12.4 0.0 collective-permute-start.2
  12.4 0.5 %collective-permute-start.3 = (bf16[1040,128]{1,0:T(8,128)(2,1)S(1)}, bf16[1040,128]{1,0:T(8,128)(2,1)S(1)}, u32[]{:S(2)}, u32[]{:S(2)}) collective-permute-start(bf16[1040,128]{1,0:T(8,128)(2,1)S(1)} %get-tuple-element.21), channel_id=1, source_target_pairs={{0,4},{4,0},{8,12},{12,8},{16,20},{20,16},{24,28},{28,24},{1,5},{5... | collective-permute-start | bytes 798728 | tf_op jit(solution)/shard_map/ppermute | solution.py:48
  12.9 3.7 %collective-permute-done.r1 = bf16[1040,128]{1,0:T(8,128)(2,1)S(1)} collective-permute-done((bf16[1040,128]{1,0:T(8,128)(2,1)S(1)}, bf16[1040,128]{1,0:T(8,128)(2,1)S(1)}, u32[]{:S(2)}, u32[]{:S(2)}) %collective-permute-start) | collective-permute-done | bytes 266272 | tf_op jit(solution)/shard_map/ppermute | solution.py:48
  16.7 2.5 %collective-permute-done.1.r2 = bf16[1040,128]{1,0:T(8,128)(2,1)S(1)} collective-permute-done((bf16[1040,128]{1,0:T(8,128)(2,1)S(1)}, bf16[1040,128]{1,0:T(8,128)(2,1)S(1)}, u32[]{:S(2)}, u32[]{:S(2)}) %collective-permute-start.1) | collective-permute-done | bytes 266272 | tf_op jit(solution)/shard_map/ppermute | solution.py:48
  19.1 0.0 collective-permute-done.2.r3
  19.1 0.0 collective-permute-done.3.r4
  19.1 0.2 average.1
  19.3 6.0 %collective-permute-start.7 = (bf16[1024,128]{1,0:T(8,128)(2,1)S(1)}, bf16[1024,128]{1,0:T(8,128)(2,1)S(1)}, u32[]{:S(2)}, u32[]{:S(2)}) collective-permute-start(bf16[1024,128]{1,0:T(8,128)(2,1)S(1)} %get-tuple-element.23.avg), channel_id=1, source_target_pairs={{0,1},{1,0},{2,3},{3,2},{4,5},{5,4},{6,7},{7,6},{8,9},{9,8},{10,11... | collective-permute-start | bytes 786440 | tf_op jit(solution)/shard_map/ppermute | solution.py:48
  25.3 0.0 collective-permute-start.6
  25.3 3.0 %collective-permute-start.5 = (bf16[1024,128]{1,0:T(8,128)(2,1)S(1)}, bf16[1024,128]{1,0:T(8,128)(2,1)S(1)}, u32[]{:S(2)}, u32[]{:S(2)}) collective-permute-start(bf16[1024,128]{1,0:T(8,128)(2,1)S(1)} %get-tuple-element.23.avg), channel_id=1, source_target_pairs={{0,28},{4,8},{8,4},{12,16},{16,12},{20,24},{24,20},{28,0},{1,29},{... | collective-permute-start | bytes 786440 | tf_op jit(solution)/shard_map/ppermute | solution.py:48
  28.4 0.0 collective-permute-start.4
  28.4 4.2 %collective-permute-done.7.r4 = bf16[1024,128]{1,0:T(8,128)(2,1)S(1)} collective-permute-done((bf16[1024,128]{1,0:T(8,128)(2,1)S(1)}, bf16[1024,128]{1,0:T(8,128)(2,1)S(1)}, u32[]{:S(2)}, u32[]{:S(2)}) %collective-permute-start.7) | collective-permute-done | bytes 262176 | tf_op jit(solution)/shard_map/ppermute | solution.py:48
  32.6 0.0 collective-permute-done.6.r3
  32.6 2.6 %collective-permute-done.5.r2 = bf16[1024,128]{1,0:T(8,128)(2,1)S(1)} collective-permute-done((bf16[1024,128]{1,0:T(8,128)(2,1)S(1)}, bf16[1024,128]{1,0:T(8,128)(2,1)S(1)}, u32[]{:S(2)}, u32[]{:S(2)}) %collective-permute-start.5) | collective-permute-done | bytes 262176 | tf_op jit(solution)/shard_map/ppermute | solution.py:48
  35.1 0.0 collective-permute-done.4.r1
  35.1 1.4 %deviation.1 = (f32[1024,128]{1,0:T(8,128)}, bf16[8,5,128,128]{3,2,1,0:T(8,128)(2,1)}) custom-call(s32[5,8]{1,0:T(8,128)S(4)} %get-tuple-element.14.at, bf16[8,5,128,128]{3,2,1,0:T(8,128)(2,1)S(1)} %get-tuple-element.15.schur, f32[1024,128]{1,0:T(8,128)S(1)} %get-tuple-element.22.mean, bf16[1024,128]{1,0:T(8,128)(2,1)S(1)} %get-tuple-element.23.avg, ...), custom_call_target="tpu_custom_call" | custom-call | tf_op jit(solution)/shard_map/deviation/pallas_call | solution.py:224
Async XLA Ops:
  7.2 9.4 %collective-permute-start = (bf16[1040,128]{1,0:T(8,128)(2,1)S(1)}, bf16[1040,128]{1,0:T(8,128)(2,1)S(1)}, u32[]{:S(2)}, u32[]{:S(2)}) collective-permute-start(bf16[1040,128]{1,0:T(8,128)(2,1)S(1)} %get-tuple-element.18), channel_id=1, source_target_pairs={{0,1},{1,0},{2,3},{3,2},{4,5},{5,4},{6,7},{7,6},{8,9},{9,8},{10,11... | collective-permute-start | bytes 798728 | tf_op jit(solution)/shard_map/ppermute | solution.py:48
  9.5 9.6 %collective-permute-start.1 = (bf16[1040,128]{1,0:T(8,128)(2,1)S(1)}, bf16[1040,128]{1,0:T(8,128)(2,1)S(1)}, u32[]{:S(2)}, u32[]{:S(2)}) collective-permute-start(bf16[1040,128]{1,0:T(8,128)(2,1)S(1)} %get-tuple-element.19), channel_id=1, source_target_pairs={{0,28},{4,8},{8,4},{12,16},{16,12},{20,24},{24,20},{28,0},{1,29},{... | collective-permute-start | bytes 798728 | tf_op jit(solution)/shard_map/ppermute | solution.py:48
  12.4 6.7 %collective-permute-start.2 = (bf16[1040,128]{1,0:T(8,128)(2,1)S(1)}, bf16[1040,128]{1,0:T(8,128)(2,1)S(1)}, u32[]{:S(2)}, u32[]{:S(2)}) collective-permute-start(bf16[1040,128]{1,0:T(8,128)(2,1)S(1)} %get-tuple-element.20), channel_id=1, source_target_pairs={{1,2},{2,1},{0,4},{3,7},{5,6},{6,5},{4,0},{7,3},{9,10},{10,9},{8,1... | collective-permute-start | bytes 798728 | tf_op jit(solution)/shard_map/ppermute | solution.py:48
  12.4 6.7 %collective-permute-start.3 = (bf16[1040,128]{1,0:T(8,128)(2,1)S(1)}, bf16[1040,128]{1,0:T(8,128)(2,1)S(1)}, u32[]{:S(2)}, u32[]{:S(2)}) collective-permute-start(bf16[1040,128]{1,0:T(8,128)(2,1)S(1)} %get-tuple-element.21), channel_id=1, source_target_pairs={{0,4},{4,0},{8,12},{12,8},{16,20},{20,16},{24,28},{28,24},{1,5},{5... | collective-permute-start | bytes 798728 | tf_op jit(solution)/shard_map/ppermute | solution.py:48
  19.3 13.2 %collective-permute-start.7 = (bf16[1024,128]{1,0:T(8,128)(2,1)S(1)}, bf16[1024,128]{1,0:T(8,128)(2,1)S(1)}, u32[]{:S(2)}, u32[]{:S(2)}) collective-permute-start(bf16[1024,128]{1,0:T(8,128)(2,1)S(1)} %get-tuple-element.23.avg), channel_id=1, source_target_pairs={{0,1},{1,0},{2,3},{3,2},{4,5},{5,4},{6,7},{7,6},{8,9},{9,8},{10,11... | collective-permute-start | bytes 786440 | tf_op jit(solution)/shard_map/ppermute | solution.py:48
  25.3 7.2 %collective-permute-start.6 = (bf16[1024,128]{1,0:T(8,128)(2,1)S(1)}, bf16[1024,128]{1,0:T(8,128)(2,1)S(1)}, u32[]{:S(2)}, u32[]{:S(2)}) collective-permute-start(bf16[1024,128]{1,0:T(8,128)(2,1)S(1)} %get-tuple-element.23.avg), channel_id=1, source_target_pairs={{0,4},{4,0},{8,12},{12,8},{16,20},{20,16},{24,28},{28,24},{1,5},{5... | collective-permute-start | bytes 786440 | tf_op jit(solution)/shard_map/ppermute | solution.py:48
  25.3 9.8 %collective-permute-start.5 = (bf16[1024,128]{1,0:T(8,128)(2,1)S(1)}, bf16[1024,128]{1,0:T(8,128)(2,1)S(1)}, u32[]{:S(2)}, u32[]{:S(2)}) collective-permute-start(bf16[1024,128]{1,0:T(8,128)(2,1)S(1)} %get-tuple-element.23.avg), channel_id=1, source_target_pairs={{0,28},{4,8},{8,4},{12,16},{16,12},{20,24},{24,20},{28,0},{1,29},{... | collective-permute-start | bytes 786440 | tf_op jit(solution)/shard_map/ppermute | solution.py:48
  28.4 6.8 %collective-permute-start.4 = (bf16[1024,128]{1,0:T(8,128)(2,1)S(1)}, bf16[1024,128]{1,0:T(8,128)(2,1)S(1)}, u32[]{:S(2)}, u32[]{:S(2)}) collective-permute-start(bf16[1024,128]{1,0:T(8,128)(2,1)S(1)} %get-tuple-element.23.avg), channel_id=1, source_target_pairs={{1,2},{2,1},{0,4},{3,7},{5,6},{6,5},{4,0},{7,3},{9,10},{10,9},{8,1... | collective-permute-start | bytes 786440 | tf_op jit(solution)/shard_map/ppermute | solution.py:48

commit v5 on v4

--- a/solution.py
+++ b/solution.py
@@ -8,8 +8,9 @@
 from jax.sharding import PartitionSpec as P
 
 PAD = 16
-SUMS_ORDER = ("near_a", "far_c", "far_a", "near_c")
-MEANS_ORDER = ("far_a", "far_c", "near_c", "near_a")
+SUMS_ORDER = ("axial_1", "far_c", "axial_2", "near_c")
+FIRST_ROWS = 2
+MEANS_ORDER = ("axial_2", "far_c", "near_c", "axial_1")
 
 
 def near_pairs(count):
@@ -27,32 +28,38 @@
     return pairs
 
 
-NAMES = ("near_c", "far_c", "near_a", "far_a")
+NAMES = ("near_c", "far_c", "axial_1", "axial_2")
+
+
+def near_first(row):
+    return row < FIRST_ROWS
 
 
 def swap_all(sent, order):
     circ, axial = lax.axis_size("circ"), lax.axis_size("axial")
+    first, second = [], []
+    for row in range(circ):
+        at = lambda i, row=row: row * axial + i
+        close = [(at(i), at(j)) for i, j in near_pairs(axial)]
+        across = [(at(i), at(j)) for i, j in far_pairs(axial, False)]
+        across += [(at(i), (row ^ 1) * axial + i) for i in (0, axial - 1)]
+        first += close if near_first(row) else across
+        second += across if near_first(row) else close
     routes = {
         "near_c": ("circ", near_pairs(circ)),
         "far_c": ("circ", far_pairs(circ, True)),
-        "near_a": ("axial", near_pairs(axial)),
-        "far_a": ("axial", far_pairs(axial, False)),
+        "axial_1": (("circ", "axial"), first),
+        "axial_2": (("circ", "axial"), second),
     }
-    diagonal = []
-    for row in range(circ):
-        for i, j in far_pairs(axial, False):
-            diagonal.append((row * axial + i, row * axial + j))
-        for i in (0, axial - 1):
-            diagonal.append((row * axial + i, (row ^ 1) * axial + i))
-    routes["far_a"] = (("circ", "axial"), diagonal)
     return [lax.ppermute(sent[name], *routes[name]) for name in order]
 
 
 def buffer_of(code):
-    odd_c = lax.rem(lax.axis_index("circ"), 2)
-    odd_a = lax.rem(lax.axis_index("axial"), 2)
-    circ = jnp.where(odd_c == 0, code, 3 - code)
-    axial = jnp.where(odd_a == 0, code, 7 - code)
+    odd_c = lax.rem(lax.axis_index("circ"), 2) == 1
+    odd_a = lax.rem(lax.axis_index("axial"), 2) == 1
+    circ = jnp.where(odd_c, 3 - code, code)
+    is_near = (code == 3) != odd_a
+    axial = jnp.where(is_near == near_first(lax.axis_index("circ")), 3, 4)
     return jnp.where(code == 0, 0, jnp.where(code <= 2, circ, axial))
 
 

time: 37 us -> 36.8 us (level)
  waiting for transfers between devices: 13 us -> 14.5 us
  starting transfers between devices: 14.7 us -> 13.6 us
    ppermute x8, waiting for transfers between devices: 13 us -> 14.5 us  [swap_all(): return [lax.ppermute(sent[name], *routes[name]) for name in order]]
    ppermute x8, starting transfers between devices: 14.7 us -> 13.6 us  [swap_all(): return [lax.ppermute(sent[name], *routes[name]) for name in order]]
where the time goes in v5:
time: 36.8 us; the launch traced here: 36.7 us
  waiting for transfers between devices  14.5 us (39%)
  starting transfers between devices  13.6 us (37%)
  Pallas kernels  7.95 us (22%)
  between operations  0.65 us (2%)
    ppermute x8, waiting for transfers between devices, swap_all(): return [lax.ppermute(sent[name], *routes[name]) for name in order]  14.5 us
    ppermute x8, starting transfers between devices, swap_all(): return [lax.ppermute(sent[name], *routes[name]) for name in order]  13.6 us
    pallas_call x1, Pallas kernels, body(): pl.pallas_call(schur_kernel, in_specs=[hbm] * 7, out_specs=[vmem] * 7 + [...  6.33 us
    pallas_call x1, Pallas kernels, body(): pl.pallas_call(functools.partial(deviation_kernel, MEANS_ORDER), in_specs...  1.43 us
  transfers between devices with their start and end apart: 8, of which 4 were waited for; matrix products, arithmetic and copies ran while one was open for 0% of the time, Pallas kernels for 0%

profile of v5, /device:TPU:0, one launch (start us, length us, event | category | flops | bytes accessed | tf_op | source)
XLA Modules:
  0.0 36.7 jit_solution(715216498120168007)
XLA Ops:
  0.6 6.3 %schur_and_sums.1 = (bf16[8,5,128,128]{3,2,1,0:T(8,128)(2,1)S(1)}, f32[1024,128]{1,0:T(8,128)S(1)}, f32[16,128]{1,0:T(8,128)S(1)}, bf16[1040,128]{1,0:T(8,128)(2...) custom-call(s32[5,1,8]{2,1,0:T(1,128)} %bitcast.18, ...), custom_call_target="tpu_custom_call" | custom-call | tf_op jit(solution)/shard_map/schur_and_sums/pallas_call | solution.py:193
  7.0 2.9 %collective-permute-start = (bf16[1040,128]{1,0:T(8,128)(2,1)S(1)}, bf16[1040,128]{1,0:T(8,128)(2,1)S(1)}, u32[]{:S(2)}, u32[]{:S(2)}) collective-permute-start(bf16[1040,128]{1,0:T(8,128)(2,1)S(1)} %get-tuple-element.18), channel_id=1, source_target_pairs={{0,1},{1,0},{2,3},{3,2},{4,5},{5,4},{6,7},{7,6},{9,10},{10,9},{8,1... | collective-permute-start | bytes 798728 | tf_op jit(solution)/shard_map/ppermute | solution.py:54
  9.9 2.9 %collective-permute-start.1 = (bf16[1040,128]{1,0:T(8,128)(2,1)S(1)}, bf16[1040,128]{1,0:T(8,128)(2,1)S(1)}, u32[]{:S(2)}, u32[]{:S(2)}) collective-permute-start(bf16[1040,128]{1,0:T(8,128)(2,1)S(1)} %get-tuple-element.19), channel_id=1, source_target_pairs={{0,28},{4,8},{8,4},{12,16},{16,12},{20,24},{24,20},{28,0},{1,29},{... | collective-permute-start | bytes 798728 | tf_op jit(solution)/shard_map/ppermute | solution.py:54
  12.8 0.0 collective-permute-start.2
  12.8 0.5 %collective-permute-start.3 = (bf16[1040,128]{1,0:T(8,128)(2,1)S(1)}, bf16[1040,128]{1,0:T(8,128)(2,1)S(1)}, u32[]{:S(2)}, u32[]{:S(2)}) collective-permute-start(bf16[1040,128]{1,0:T(8,128)(2,1)S(1)} %get-tuple-element.21), channel_id=1, source_target_pairs={{0,4},{4,0},{8,12},{12,8},{16,20},{20,16},{24,28},{28,24},{1,5},{5... | collective-permute-start | bytes 798728 | tf_op jit(solution)/shard_map/ppermute | solution.py:54
  13.3 3.9 %collective-permute-done.r1 = bf16[1040,128]{1,0:T(8,128)(2,1)S(1)} collective-permute-done((bf16[1040,128]{1,0:T(8,128)(2,1)S(1)}, bf16[1040,128]{1,0:T(8,128)(2,1)S(1)}, u32[]{:S(2)}, u32[]{:S(2)}) %collective-permute-start) | collective-permute-done | bytes 266272 | tf_op jit(solution)/shard_map/ppermute | solution.py:54
  17.1 2.8 %collective-permute-done.1.r2 = bf16[1040,128]{1,0:T(8,128)(2,1)S(1)} collective-permute-done((bf16[1040,128]{1,0:T(8,128)(2,1)S(1)}, bf16[1040,128]{1,0:T(8,128)(2,1)S(1)}, u32[]{:S(2)}, u32[]{:S(2)}) %collective-permute-start.1) | collective-permute-done | bytes 266272 | tf_op jit(solution)/shard_map/ppermute | solution.py:54
  20.0 0.0 collective-permute-done.2.r3
  20.0 0.0 collective-permute-done.3.r4
  20.0 0.2 average.1
  20.2 4.9 %collective-permute-start.7 = (bf16[1024,128]{1,0:T(8,128)(2,1)S(1)}, bf16[1024,128]{1,0:T(8,128)(2,1)S(1)}, u32[]{:S(2)}, u32[]{:S(2)}) collective-permute-start(bf16[1024,128]{1,0:T(8,128)(2,1)S(1)} %get-tuple-element.23.avg), channel_id=1, source_target_pairs={{0,1},{1,0},{2,3},{3,2},{4,5},{5,4},{6,7},{7,6},{9,10},{10,9},{8,1... | collective-permute-start | bytes 786440 | tf_op jit(solution)/shard_map/ppermute | solution.py:54
  25.1 0.0 collective-permute-start.6
  25.1 2.3 %collective-permute-start.5 = (bf16[1024,128]{1,0:T(8,128)(2,1)S(1)}, bf16[1024,128]{1,0:T(8,128)(2,1)S(1)}, u32[]{:S(2)}, u32[]{:S(2)}) collective-permute-start(bf16[1024,128]{1,0:T(8,128)(2,1)S(1)} %get-tuple-element.23.avg), channel_id=1, source_target_pairs={{0,28},{4,8},{8,4},{12,16},{16,12},{20,24},{24,20},{28,0},{1,29},{... | collective-permute-start | bytes 786440 | tf_op jit(solution)/shard_map/ppermute | solution.py:54
  27.4 0.0 collective-permute-start.4
  27.4 4.3 %collective-permute-done.7.r4 = bf16[1024,128]{1,0:T(8,128)(2,1)S(1)} collective-permute-done((bf16[1024,128]{1,0:T(8,128)(2,1)S(1)}, bf16[1024,128]{1,0:T(8,128)(2,1)S(1)}, u32[]{:S(2)}, u32[]{:S(2)}) %collective-permute-start.7) | collective-permute-done | bytes 262176 | tf_op jit(solution)/shard_map/ppermute | solution.py:54
  31.7 0.0 collective-permute-done.6.r3
  31.7 3.6 %collective-permute-done.5.r2 = bf16[1024,128]{1,0:T(8,128)(2,1)S(1)} collective-permute-done((bf16[1024,128]{1,0:T(8,128)(2,1)S(1)}, bf16[1024,128]{1,0:T(8,128)(2,1)S(1)}, u32[]{:S(2)}, u32[]{:S(2)}) %collective-permute-start.5) | collective-permute-done | bytes 262176 | tf_op jit(solution)/shard_map/ppermute | solution.py:54
  35.3 0.0 collective-permute-done.4.r1
  35.3 1.4 %deviation.1 = (f32[1024,128]{1,0:T(8,128)}, bf16[8,5,128,128]{3,2,1,0:T(8,128)(2,1)}) custom-call(s32[5,8]{1,0:T(8,128)S(4)} %get-tuple-element.14.at, bf16[8,5,128,128]{3,2,1,0:T(8,128)(2,1)S(1)} %get-tuple-element.15.schur, f32[1024,128]{1,0:T(8,128)S(1)} %get-tuple-element.22.mean, bf16[1024,128]{1,0:T(8,128)(2,1)S(1)} %get-tuple-element.23.avg, ...), custom_call_target="tpu_custom_call" | custom-call | tf_op jit(solution)/shard_map/deviation/pallas_call | solution.py:231
Async XLA Ops:
  7.0 10.2 %collective-permute-start = (bf16[1040,128]{1,0:T(8,128)(2,1)S(1)}, bf16[1040,128]{1,0:T(8,128)(2,1)S(1)}, u32[]{:S(2)}, u32[]{:S(2)}) collective-permute-start(bf16[1040,128]{1,0:T(8,128)(2,1)S(1)} %get-tuple-element.18), channel_id=1, source_target_pairs={{0,1},{1,0},{2,3},{3,2},{4,5},{5,4},{6,7},{7,6},{9,10},{10,9},{8,1... | collective-permute-start | bytes 798728 | tf_op jit(solution)/shard_map/ppermute | solution.py:54
  9.9 10.1 %collective-permute-start.1 = (bf16[1040,128]{1,0:T(8,128)(2,1)S(1)}, bf16[1040,128]{1,0:T(8,128)(2,1)S(1)}, u32[]{:S(2)}, u32[]{:S(2)}) collective-permute-start(bf16[1040,128]{1,0:T(8,128)(2,1)S(1)} %get-tuple-element.19), channel_id=1, source_target_pairs={{0,28},{4,8},{8,4},{12,16},{16,12},{20,24},{24,20},{28,0},{1,29},{... | collective-permute-start | bytes 798728 | tf_op jit(solution)/shard_map/ppermute | solution.py:54
  12.8 7.2 %collective-permute-start.2 = (bf16[1040,128]{1,0:T(8,128)(2,1)S(1)}, bf16[1040,128]{1,0:T(8,128)(2,1)S(1)}, u32[]{:S(2)}, u32[]{:S(2)}) collective-permute-start(bf16[1040,128]{1,0:T(8,128)(2,1)S(1)} %get-tuple-element.20), channel_id=1, source_target_pairs={{1,2},{2,1},{0,4},{3,7},{5,6},{6,5},{4,0},{7,3},{8,9},{9,8},{10,11... | collective-permute-start | bytes 798728 | tf_op jit(solution)/shard_map/ppermute | solution.py:54
  12.8 7.2 %collective-permute-start.3 = (bf16[1040,128]{1,0:T(8,128)(2,1)S(1)}, bf16[1040,128]{1,0:T(8,128)(2,1)S(1)}, u32[]{:S(2)}, u32[]{:S(2)}) collective-permute-start(bf16[1040,128]{1,0:T(8,128)(2,1)S(1)} %get-tuple-element.21), channel_id=1, source_target_pairs={{0,4},{4,0},{8,12},{12,8},{16,20},{20,16},{24,28},{28,24},{1,5},{5... | collective-permute-start | bytes 798728 | tf_op jit(solution)/shard_map/ppermute | solution.py:54
  20.2 11.5 %collective-permute-start.7 = (bf16[1024,128]{1,0:T(8,128)(2,1)S(1)}, bf16[1024,128]{1,0:T(8,128)(2,1)S(1)}, u32[]{:S(2)}, u32[]{:S(2)}) collective-permute-start(bf16[1024,128]{1,0:T(8,128)(2,1)S(1)} %get-tuple-element.23.avg), channel_id=1, source_target_pairs={{0,1},{1,0},{2,3},{3,2},{4,5},{5,4},{6,7},{7,6},{9,10},{10,9},{8,1... | collective-permute-start | bytes 786440 | tf_op jit(solution)/shard_map/ppermute | solution.py:54
  25.1 6.6 %collective-permute-start.6 = (bf16[1024,128]{1,0:T(8,128)(2,1)S(1)}, bf16[1024,128]{1,0:T(8,128)(2,1)S(1)}, u32[]{:S(2)}, u32[]{:S(2)}) collective-permute-start(bf16[1024,128]{1,0:T(8,128)(2,1)S(1)} %get-tuple-element.23.avg), channel_id=1, source_target_pairs={{0,4},{4,0},{8,12},{12,8},{16,20},{20,16},{24,28},{28,24},{1,5},{5... | collective-permute-start | bytes 786440 | tf_op jit(solution)/shard_map/ppermute | solution.py:54
  25.1 10.2 %collective-permute-start.5 = (bf16[1024,128]{1,0:T(8,128)(2,1)S(1)}, bf16[1024,128]{1,0:T(8,128)(2,1)S(1)}, u32[]{:S(2)}, u32[]{:S(2)}) collective-permute-start(bf16[1024,128]{1,0:T(8,128)(2,1)S(1)} %get-tuple-element.23.avg), channel_id=1, source_target_pairs={{0,28},{4,8},{8,4},{12,16},{16,12},{20,24},{24,20},{28,0},{1,29},{... | collective-permute-start | bytes 786440 | tf_op jit(solution)/shard_map/ppermute | solution.py:54
  27.4 7.8 %collective-permute-start.4 = (bf16[1024,128]{1,0:T(8,128)(2,1)S(1)}, bf16[1024,128]{1,0:T(8,128)(2,1)S(1)}, u32[]{:S(2)}, u32[]{:S(2)}) collective-permute-start(bf16[1024,128]{1,0:T(8,128)(2,1)S(1)} %get-tuple-element.23.avg), channel_id=1, source_target_pairs={{1,2},{2,1},{0,4},{3,7},{5,6},{6,5},{4,0},{7,3},{8,9},{9,8},{10,11... | collective-permute-start | bytes 786440 | tf_op jit(solution)/shard_map/ppermute | solution.py:54
